TPU v7x, 128 devices: a whole 4x4x4 slice. The times are simulated.
128 devices in a mesh: rep: 16 (over x, y), shard: 8 (over z, core).
Axes of the slice: x: 4, y: 4, z: 4, core: 2. Of those that a mesh axis runs over, the one named last changes fastest.
Arguments:
- tokens: bfloat16 [16384, 1024], P(('rep', 'shard')), may hold values from -24 to 24
- cotangent: bfloat16 [16384, 1024], P(('rep', 'shard')), may hold values from -6 to 6
- lengths: int32 [16, 3], P('rep'), may hold values from 1 to 898, 1024 in all within a row
- qkv_proj: float32 [1024, 2048], P(('rep', 'shard')), may hold values from -0.1875 to 0.1875
- out_proj: float32 [1024, 1024], P(('rep', 'shard')), may hold values from -3 to 3
- gate_proj: float32 [1024, 9216], P(('rep', 'shard')), may hold values from -0.1875 to 0.1875
- down_proj: float32 [4608, 1024], P(('rep', 'shard')), may hold values from -0.09375 to 0.09375
- norm_gains: float32 [2176], P(('rep', 'shard')), may hold values from 0.5 to 1.5
- qkv_first: float32 [1024, 2048], P(('rep', 'shard')), may hold values from -40 to 40
- out_first: float32 [1024, 1024], P(('rep', 'shard')), may hold values from -6 to 6
- gate_first: float32 [1024, 9216], P(('rep', 'shard')), may hold values from -24 to 24
- down_first: float32 [4608, 1024], P(('rep', 'shard')), may hold values from -48 to 48
- gain_first: float32 [2176], P(('rep', 'shard')), may hold values from -64 to 64
- qkv_second: float32 [1024, 2048], P(('rep', 'shard')), may hold values from 212.992 to 868.352
- out_second: float32 [1024, 1024], P(('rep', 'shard')), may hold values from 4.16 to 16.8
- gate_second: float32 [1024, 9216], P(('rep', 'shard')), may hold values from 62.2592 to 245.76
- down_second: float32 [4608, 1024], P(('rep', 'shard')), may hold values from 311.296 to 1245.184
- gain_second: float32 [2176], P(('rep', 'shard')), may hold values from 425.984 to 1638.4
Outputs:
- block_output: float32 [16384, 1024], P(('rep', 'shard'))
- input_grad: float32 [16384, 1024], P(('rep', 'shard'))
- qkv_next: float32 [1024, 2048], P(('rep', 'shard'))
- qkv_mean: float32 [1024, 2048], P(('rep', 'shard'))
- qkv_square: float32 [1024, 2048], P(('rep', 'shard'))
- out_next: float32 [1024, 1024], P(('rep', 'shard'))
- out_mean: float32 [1024, 1024], P(('rep', 'shard'))
- out_square: float32 [1024, 1024], P(('rep', 'shard'))
- gate_next: float32 [1024, 9216], P(('rep', 'shard'))
- gate_mean: float32 [1024, 9216], P(('rep', 'shard'))
- gate_square: float32 [1024, 9216], P(('rep', 'shard'))
- down_next: float32 [4608, 1024], P(('rep', 'shard'))
- down_mean: float32 [4608, 1024], P(('rep', 'shard'))
- down_square: float32 [4608, 1024], P(('rep', 'shard'))
- gain_next: float32 [2176], P(('rep', 'shard'))
- gain_mean: float32 [2176], P(('rep', 'shard'))
- gain_square: float32 [2176], P(('rep', 'shard'))
Inputs may be any that keep to these rules, and one draw needn't show every extreme that they name: Each row holds the 3 lengths of the documents packed in order into one sequence; they sum to 1024, and one of them is exactly 898.
All inputs are finite; a program needn't handle non-finite values.
Results may differ from a plain program's by a relative error of at most 0.02.
Values may be sent and summed in bfloat16 or wider, within the bound.
No kernel may reach another device: no remote copies, remote signals or barrier semaphores. Data moves between devices by JAX's collectives and lax.ppermute only.
A program may use at most 192 MiB of HBM per device.

v0:
```python
import jax
import jax.numpy as jnp
from jax import lax
from jax.sharding import PartitionSpec as P

D = 1024
FF = 4608
HQ = 16
KEY_VALUE_HEADS = 8
HEAD_SIZE = 64
STEP = 10
QUERY_FEATURES = 1024
KEY_FEATURES = 512
QUERY_PER_KEY = 2
WO_FAN = 4


norm_eps = 1e-05
theta = 1000000.0
beta_one = 0.9
beta_two = 0.95
adam_eps = 1e-08
decay = 0.1
rate_scale = 2.0
gain_rate = 1.0
masked_score = -1e30


def norm_pieces_list(field):
    scale = lax.rsqrt(jnp.mean(field * field, axis=-1, keepdims=True) + norm_eps)
    return (field * scale, scale)


def norm_back(incoming_grad, normed, scale, gain):
    gain_grad = jnp.sum((incoming_grad * normed).reshape(-1, normed.shape[-1]), axis=0)
    scaled = incoming_grad * gain
    inner = jnp.mean(scaled * normed, axis=-1, keepdims=True)
    return (gain_grad, scale * (scaled - normed * inner))


def document_info(lengths_row, index):
    ends = jnp.cumsum(lengths_row)
    passed = ends[None, :] <= index[:, None]
    docs = jnp.sum(passed.astype(jnp.int32), axis=1)
    starts = jnp.sum(jnp.where(passed, lengths_row[None, :], 0), axis=1)
    return (docs, index - starts)


def rotation_tables(places):
    half = HEAD_SIZE // 2
    freqs = theta ** (-(jnp.arange(half, dtype=jnp.float32) * 2.0) / HEAD_SIZE)
    angles = places.astype(jnp.float32)[:, None] * freqs[None, :]
    return (jnp.cos(angles), jnp.sin(angles))


def apply_rotary(field, cosine_table, sine_table):
    half = field.shape[-1] // 2
    first = field[..., :half]
    second = field[..., half:]
    cos_rows = cosine_table[:, None, :]
    sin_rows = sine_table[:, None, :]
    return jnp.concatenate(
        [first * cos_rows - second * sin_rows, second * cos_rows + first * sin_rows], axis=-1
    )


def rotary_inverse(field, cosine_table, sine_table):
    half = field.shape[-1] // 2
    first = field[..., :half]
    second = field[..., half:]
    cos_rows = cosine_table[:, None, :]
    sin_rows = sine_table[:, None, :]
    return jnp.concatenate(
        [first * cos_rows + second * sin_rows, second * cos_rows - first * sin_rows], axis=-1
    )


def block_scores(query, key_rows, key_docs, query_docs, query_index, start, block):
    key_block = lax.dynamic_slice_in_dim(key_rows, start, block, 0)
    doc_block = lax.dynamic_slice_in_dim(key_docs, start, block, 0)
    raw = jnp.einsum(
        "tgjd,sgd->gjts", query, key_block, preferred_element_type=jnp.float32
    ) * HEAD_SIZE ** (-0.5)
    block_index = start + jnp.arange(block, dtype=jnp.int32)
    allowed = (block_index[None, :] <= query_index[:, None]) & (
        doc_block[None, :] == query_docs[:, None]
    )
    return (raw, allowed)


def attention_forward(
    query, key_rows, value_rows, key_docs, query_docs, query_index, block, nblocks
):
    token_rows = query.shape[0]
    shape = (query.shape[1], query.shape[2], token_rows)

    def max_sum(step, carry):
        top, total = carry
        raw, allowed = block_scores(
            query, key_rows, key_docs, query_docs, query_index, step * block, block
        )
        masked = jnp.where(allowed, raw, masked_score)
        new_top = jnp.maximum(top, jnp.max(masked, axis=-1))
        weight = jnp.where(allowed, jnp.exp(masked - new_top[..., None]), 0.0)
        return (new_top, total * jnp.exp(top - new_top) + jnp.sum(weight, axis=-1))

    start_top = jnp.full(shape, masked_score, jnp.float32)
    top, total = lax.fori_loop(0, nblocks, max_sum, (start_top, jnp.zeros(shape, jnp.float32)))
    shift = top + jnp.log(total)

    def weighted(step, carry):
        main, extra = carry
        start = step * block
        raw, allowed = block_scores(
            query, key_rows, key_docs, query_docs, query_index, start, block
        )
        probs = jnp.where(allowed, jnp.exp(raw - shift[..., None]), 0.0)
        low_probs = probs.astype(jnp.bfloat16)
        remains = (probs - low_probs.astype(jnp.float32)).astype(jnp.bfloat16)
        value_block = lax.dynamic_slice_in_dim(value_rows, start, block, 0)
        main = main + jnp.einsum(
            "gjts,sgd->gjtd", low_probs, value_block, preferred_element_type=jnp.float32
        )
        extra = extra + jnp.einsum(
            "gjts,sgd->gjtd", remains, value_block, preferred_element_type=jnp.float32
        )
        return (main, extra)

    empty = jnp.zeros(shape + (query.shape[3],), jnp.float32)
    main, extra = lax.fori_loop(0, nblocks, weighted, (empty, empty))
    return (main, extra, shift)


def attention_backward(
    query,
    key_rows,
    value_rows,
    incoming_grad,
    spread,
    shift,
    key_docs,
    query_docs,
    query_index,
    block,
    nblocks,
):

    def accumulate(step, carry):
        query_grad, key_grad, value_grad = carry
        start = step * block
        raw, allowed = block_scores(
            query, key_rows, key_docs, query_docs, query_index, start, block
        )
        probs = jnp.where(allowed, jnp.exp(raw - shift[..., None]), 0.0)
        low_probs = probs.astype(jnp.bfloat16)
        key_block = lax.dynamic_slice_in_dim(key_rows, start, block, 0)
        value_block = lax.dynamic_slice_in_dim(value_rows, start, block, 0)
        prob_grad = jnp.einsum(
            "tgjd,sgd->gjts", incoming_grad, value_block, preferred_element_type=jnp.float32
        )
        score_grad = (probs * (prob_grad - spread[..., None])).astype(jnp.bfloat16)
        query_grad = query_grad + jnp.einsum(
            "gjts,sgd->tgjd", score_grad, key_block, preferred_element_type=jnp.float32
        ) * HEAD_SIZE ** (-0.5)
        key_part = jnp.einsum(
            "gjts,tgjd->sgd", score_grad, query, preferred_element_type=jnp.float32
        ) * HEAD_SIZE ** (-0.5)
        value_part = jnp.einsum(
            "gjts,tgjd->sgd", low_probs, incoming_grad, preferred_element_type=jnp.float32
        )
        key_grad = lax.dynamic_update_slice_in_dim(
            key_grad, lax.dynamic_slice_in_dim(key_grad, start, block, 0) + key_part, start, 0
        )
        value_grad = lax.dynamic_update_slice_in_dim(
            value_grad, lax.dynamic_slice_in_dim(value_grad, start, block, 0) + value_part, start, 0
        )
        return (query_grad, key_grad, value_grad)

    start_query = jnp.zeros(query.shape, jnp.float32)
    start_keys = jnp.zeros(key_rows.shape, jnp.float32)
    return lax.fori_loop(0, nblocks, accumulate, (start_query, start_keys, start_keys))


def adamw(weight, grad, first, second, rate, weight_decay):
    new_first = beta_one * first + (1.0 - beta_one) * grad
    new_second = beta_two * second + (1.0 - beta_two) * grad * grad
    step_size = (
        new_first
        / (1.0 - beta_one**STEP)
        / (jnp.sqrt(new_second / (1.0 - beta_two**STEP)) + adam_eps)
    )
    return (weight - rate * (step_size + weight_decay * weight), new_first, new_second)


def local(
    tokens,
    cotangent,
    lengths,
    qkv_proj,
    out_proj,
    gate_proj,
    down_proj,
    norm_gains,
    qkv_first,
    out_first,
    gate_first,
    down_first,
    gain_first,
    qkv_second,
    out_second,
    gate_second,
    down_second,
    gain_second,
):
    qkv_low = qkv_proj.astype(jnp.bfloat16)
    out_low = out_proj.astype(jnp.bfloat16)
    gate_low = gate_proj.astype(jnp.bfloat16)
    down_low = down_proj.astype(jnp.bfloat16)
    gain_low = norm_gains.astype(jnp.bfloat16)
    whole = (
        lax.all_gather(qkv_low, ("rep", "shard"), axis=0, tiled=True),
        lax.all_gather(out_low, ("rep", "shard"), axis=0, tiled=True),
        lax.all_gather(gate_low, ("rep", "shard"), axis=0, tiled=True),
        lax.all_gather(down_low, ("rep", "shard"), axis=0, tiled=True),
        lax.all_gather(gain_low, ("rep", "shard"), axis=0, tiled=True),
    )
    qkv_w, out_w, gate_w, down_w, gain_w = whole
    gains = gain_w.astype(jnp.float32)
    gain_attn = gains[:D]
    query_norm_gain = gains[D : D + HEAD_SIZE]
    gain_key = gains[D + HEAD_SIZE : D + 2 * HEAD_SIZE]
    gain_ffn = gains[D + 2 * HEAD_SIZE :]
    token_rows = tokens.shape[0]
    sequence_length = token_rows * lax.axis_size("shard")
    block = min(512, sequence_length)
    shard_pos = lax.axis_index("shard")
    query_index = shard_pos * token_rows + jnp.arange(token_rows, dtype=jnp.int32)
    lengths_row = lengths[0]
    query_docs, query_places = document_info(lengths_row, query_index)
    key_docs = document_info(lengths_row, jnp.arange(sequence_length, dtype=jnp.int32))[0]
    cosine_table, sine_table = rotation_tables(query_places)
    nblocks = ((shard_pos + 1) * token_rows + block - 1) // block
    inputs = tokens.astype(jnp.float32)
    input_hat, input_scale = norm_pieces_list(inputs)
    normed = (input_hat * gain_attn).astype(jnp.bfloat16)
    projected_rows = jnp.dot(normed, qkv_w, preferred_element_type=jnp.float32)
    query_hat, query_scale = norm_pieces_list(
        projected_rows[:, :QUERY_FEATURES].reshape(token_rows, HQ, HEAD_SIZE)
    )
    key_normalized, key_inverse_norm = norm_pieces_list(
        projected_rows[:, QUERY_FEATURES : QUERY_FEATURES + KEY_FEATURES].reshape(
            token_rows, KEY_VALUE_HEADS, HEAD_SIZE
        )
    )
    value_own = projected_rows[:, QUERY_FEATURES + KEY_FEATURES :].astype(jnp.bfloat16)
    query = (
        apply_rotary(query_hat * query_norm_gain, cosine_table, sine_table)
        .astype(jnp.bfloat16)
        .reshape(token_rows, KEY_VALUE_HEADS, QUERY_PER_KEY, HEAD_SIZE)
    )
    key_own = (
        apply_rotary(key_normalized * gain_key, cosine_table, sine_table)
        .astype(jnp.bfloat16)
        .reshape(token_rows, KEY_FEATURES)
    )
    key_full_shard, value_full_shard = (
        lax.all_gather(key_own, "shard", axis=0, tiled=True),
        lax.all_gather(value_own, "shard", axis=0, tiled=True),
    )
    key_rows = key_full_shard.reshape(sequence_length, KEY_VALUE_HEADS, HEAD_SIZE)
    value_rows = value_full_shard.reshape(sequence_length, KEY_VALUE_HEADS, HEAD_SIZE)
    main, extra, shift = attention_forward(
        query, key_rows, value_rows, key_docs, query_docs, query_index, block, nblocks
    )
    mixed = (
        jnp.transpose(main, (2, 0, 1, 3)).reshape(token_rows, QUERY_FEATURES).astype(jnp.bfloat16)
    )
    residual = inputs + jnp.dot(mixed, out_w, preferred_element_type=jnp.float32)
    residual_hat, residual_scale = norm_pieces_list(residual)
    normed_two = (residual_hat * gain_ffn).astype(jnp.bfloat16)
    both = jnp.dot(normed_two, gate_w, preferred_element_type=jnp.float32)
    gate = both[:, :FF]
    upper = both[:, FF:]
    sigmoid_gate = jax.nn.sigmoid(gate)
    activated = gate * sigmoid_gate
    hidden = (activated * upper).astype(jnp.bfloat16)
    block_output = residual + jnp.dot(hidden, down_w, preferred_element_type=jnp.float32)
    down_grad = jnp.einsum("tf,td->fd", hidden, cotangent, preferred_element_type=jnp.float32)
    hidden_grad = jnp.einsum("td,fd->tf", cotangent, down_w, preferred_element_type=jnp.float32)
    both_grad = jnp.concatenate(
        [
            hidden_grad * upper * sigmoid_gate * (1.0 + gate * (1.0 - sigmoid_gate)),
            hidden_grad * activated,
        ],
        axis=1,
    ).astype(jnp.bfloat16)
    gate_grad = jnp.einsum("td,tf->df", normed_two, both_grad, preferred_element_type=jnp.float32)
    normed_two_grad = jnp.einsum("tf,df->td", both_grad, gate_w, preferred_element_type=jnp.float32)
    gain_ffn_grad, residual_part = norm_back(
        normed_two_grad, residual_hat, residual_scale, gain_ffn
    )
    residual_grad = cotangent.astype(jnp.float32) + residual_part
    branch_grad = residual_grad.astype(jnp.bfloat16)
    out_grad = jnp.einsum("tq,td->qd", mixed, branch_grad, preferred_element_type=jnp.float32)
    combined_grad = jnp.einsum(
        "td,qd->tq", branch_grad, out_w, preferred_element_type=jnp.float32
    ).astype(jnp.bfloat16)
    incoming_grad = combined_grad.reshape(token_rows, KEY_VALUE_HEADS, QUERY_PER_KEY, HEAD_SIZE)
    spread = jnp.sum(
        jnp.transpose(incoming_grad.astype(jnp.float32), (1, 2, 0, 3)) * (main + extra), axis=-1
    )
    key_recomputed, value_recomputed = (
        lax.all_gather(key_own, "shard", axis=0, tiled=True),
        lax.all_gather(value_own, "shard", axis=0, tiled=True),
    )
    key_rows_grad = key_recomputed.reshape(sequence_length, KEY_VALUE_HEADS, HEAD_SIZE)
    value_rows_grad = value_recomputed.reshape(sequence_length, KEY_VALUE_HEADS, HEAD_SIZE)
    query_grad, key_grad_all, value_grad_all = attention_backward(
        query,
        key_rows_grad,
        value_rows_grad,
        incoming_grad,
        spread,
        shift,
        key_docs,
        query_docs,
        query_index,
        block,
        nblocks,
    )
    key_grad_local, value_grad_own = (
        lax.psum_scatter(
            key_grad_all.reshape(sequence_length, KEY_FEATURES).astype(jnp.bfloat16),
            "shard",
            scatter_dimension=0,
            tiled=True,
        ).astype(jnp.float32),
        lax.psum_scatter(
            value_grad_all.reshape(sequence_length, KEY_FEATURES).astype(jnp.bfloat16),
            "shard",
            scatter_dimension=0,
            tiled=True,
        ).astype(jnp.float32),
    )
    query_back = rotary_inverse(
        query_grad.reshape(token_rows, HQ, HEAD_SIZE), cosine_table, sine_table
    )
    gain_query_grad, query_proj_grad = norm_back(
        query_back, query_hat, query_scale, query_norm_gain
    )
    key_unrotated_grad = rotary_inverse(
        key_grad_local.reshape(token_rows, KEY_VALUE_HEADS, HEAD_SIZE), cosine_table, sine_table
    )
    gain_key_grad, key_proj_grad = norm_back(
        key_unrotated_grad, key_normalized, key_inverse_norm, gain_key
    )
    projected_grad = jnp.concatenate(
        [
            query_proj_grad.reshape(token_rows, QUERY_FEATURES).astype(jnp.bfloat16),
            key_proj_grad.reshape(token_rows, KEY_FEATURES).astype(jnp.bfloat16),
            value_grad_own.astype(jnp.bfloat16),
        ],
        axis=1,
    )
    qkv_grad = jnp.einsum("td,tc->dc", normed, projected_grad, preferred_element_type=jnp.float32)
    normed_grad = jnp.einsum("tc,dc->td", projected_grad, qkv_w, preferred_element_type=jnp.float32)
    gain_attn_grad, input_part = norm_back(normed_grad, input_hat, input_scale, gain_attn)
    input_grad = residual_grad + input_part
    gain_grad = jnp.concatenate([gain_attn_grad, gain_query_grad, gain_key_grad, gain_ffn_grad])
    reduced = (
        lax.psum_scatter(qkv_grad, ("rep", "shard"), scatter_dimension=0, tiled=True),
        lax.psum_scatter(out_grad, ("rep", "shard"), scatter_dimension=0, tiled=True),
        lax.psum_scatter(gate_grad, ("rep", "shard"), scatter_dimension=0, tiled=True),
        lax.psum_scatter(down_grad, ("rep", "shard"), scatter_dimension=0, tiled=True),
        lax.psum_scatter(gain_grad, ("rep", "shard"), scatter_dimension=0, tiled=True),
    )
    masters = (qkv_proj, out_proj, gate_proj, down_proj, norm_gains)
    firsts = (qkv_first, out_first, gate_first, down_first, gain_first)
    seconds = (qkv_second, out_second, gate_second, down_second, gain_second)
    rates = (
        rate_scale * D ** (-0.5),
        rate_scale * WO_FAN ** (-0.5),
        rate_scale * D ** (-0.5),
        rate_scale * FF ** (-0.5),
        gain_rate,
    )
    decays = (decay, decay, decay, decay, 0.0)
    results = []
    for number in range(5):
        results.extend(
            adamw(
                masters[number],
                reduced[number],
                firsts[number],
                seconds[number],
                rates[number],
                decays[number],
            )
        )
    return (
        block_output,
        input_grad,
        results[0],
        results[1],
        results[2],
        results[3],
        results[4],
        results[5],
        results[6],
        results[7],
        results[8],
        results[9],
        results[10],
        results[11],
        results[12],
        results[13],
        results[14],
    )


def solution(mesh):
    return jax.shard_map(
        local,
        mesh=mesh,
        in_specs=(
            P(("rep", "shard"), None),
            P(("rep", "shard"), None),
            P("rep", None),
            P(("rep", "shard"), None),
            P(("rep", "shard"), None),
            P(("rep", "shard"), None),
            P(("rep", "shard"), None),
            P(("rep", "shard")),
            P(("rep", "shard"), None),
            P(("rep", "shard"), None),
            P(("rep", "shard"), None),
            P(("rep", "shard"), None),
            P(("rep", "shard")),
            P(("rep", "shard"), None),
            P(("rep", "shard"), None),
            P(("rep", "shard"), None),
            P(("rep", "shard"), None),
            P(("rep", "shard")),
        ),
        out_specs=(
            P(("rep", "shard"), None),
            P(("rep", "shard"), None),
            P(("rep", "shard"), None),
            P(("rep", "shard"), None),
            P(("rep", "shard"), None),
            P(("rep", "shard"), None),
            P(("rep", "shard"), None),
            P(("rep", "shard"), None),
            P(("rep", "shard"), None),
            P(("rep", "shard"), None),
            P(("rep", "shard"), None),
            P(("rep", "shard"), None),
            P(("rep", "shard"), None),
            P(("rep", "shard"), None),
            P(("rep", "shard")),
            P(("rep", "shard")),
            P(("rep", "shard")),
        ),
        check_vma=False,
    )
```

profile of v0, /device:TPU:1, one launch (start us, length us, event | category | flops | bytes accessed | tf_op | source)
XLA Modules:
  0.0 2048.2 jit_solution(12499207011295319423)
XLA Ops:
  9.6 69.3 %all-reduce = bf16[2176]{0:T(1024)(128)(2,1)S(1)} all-reduce(bf16[2176]{0:T(1024)(128)(2,1)S(1)} %dynamic-update-slice), channel_id=1, replica_groups=mesh['rep'=16,'shard'=8] {'rep','shard'}, use_global_device_ids=true, to_apply=%add | all-reduce | flops 2176 | bytes 8704
  80.1 2.2 all-gather.8.cloned.1.call-done
  82.3 3.1 fusion.104
  91.3 16.2 all-gather.12.cloned.1.call-done
  109.0 24.2 %all-gather.10.cloned.1.call-done = bf16[1024,512]{0,1:T(8,128)(2,1)} async-done(((bf16[128,512]{0,1:T(8,128)(2,1)}), bf16[1024,512]{0,1:T(8,128)(2,1)}) %all-gather.10.cloned.1.call-update) | async-done | bytes 1048592 | tf_op jit(solution)/shard_map/all_gather | solution.py:267
  133.2 3.2 while.41
  133.6 1.9 fusion.172
  136.6 4.5 while.42
  136.9 1.8 fusion.178
  141.2 61.8 %all-gather.14.cloned.1.call-done = bf16[1024,1024]{1,0:T(8,128)(2,1)} async-done(((bf16[8,1024]{1,0:T(8,128)(2,1)}), bf16[1024,1024]{1,0:T(8,128)(2,1)}) %all-gather.14.cloned.1.call-update) | async-done | bytes 2097168 | tf_op jit(solution)/shard_map/all_gather | solution.py:222
  203.0 2.1 multiply_reduce_fusion.3
  205.1 70.5 %all-gather.18.cloned.1.call-done = bf16[128,36,1024]{2,1,0:T(8,128)(2,1)} async-done(((bf16[1,36,1024]{2,1,0:T(8,128)(2,1)}), bf16[128,36,1024]{2,1,0:T(8,128)(2,1)}) %all-gather.18.cloned.1.call-update) | async-done | bytes 9437200 | tf_op jit(solution)/shard_map/all_gather | solution.py:224
  275.6 13.1 reshape.296
  288.7 71.8 %all-gather.16.cloned.1.call-done = bf16[1024,9216]{1,0:T(8,128)(2,1)} async-done(((bf16[8,9216]{1,0:T(8,128)(2,1)}), bf16[1024,9216]{1,0:T(8,128)(2,1)}) %all-gather.16.cloned.1.call-update) | async-done | bytes 18874384 | tf_op jit(solution)/shard_map/all_gather | solution.py:223
  360.6 8.0 fusion.115
  369.6 5.0 multiply_convert_fusion.1
  374.7 11.8 multiply_reduce_fusion
  391.4 5.4 while.43
  401.8 2.7 fusion.100
  410.5 21.5 %reduce-scatter.18.cloned.1.call-done = bf16[128,512]{1,0:T(8,128)(2,1)} async-done(((bf16[1024,512]{1,0:T(8,128)(2,1)}), bf16[128,512]{1,0:T(8,128)(2,1)}) %reduce-scatter.18.cloned.1.call-update) | async-done | bytes 131088
  436.1 29.1 %reduce-scatter.10.cloned.1.call-done = bf16[128,512]{1,0:T(8,128)(2,1)} async-done(((bf16[1024,512]{1,0:T(8,128)(2,1)}), bf16[128,512]{1,0:T(8,128)(2,1)}) %reduce-scatter.10.cloned.1.call-update) | async-done | bytes 131088 | tf_op jit(solution)/shard_map/reduce_scatter | solution.py:338
  465.2 5.5 fusion.97
  472.1 16.1 fusion.80
  489.6 7.8 fusion.123
  497.3 364.3 %fusion.6 = f32[40,1024]{1,0:T(8,128)} fusion(f32[4608,1024]{1,0:T(8,128)} %fusion.123), kind=kCustom, calls=%all-reduce-scatter | all-reduce-scatter fusion | flops 5242881 | bytes 19038208
  863.0 2.0 collective-permute-start.10
  866.5 1.9 collective-permute-start.12
  871.0 2.1 collective-permute-start.9
  873.1 1.9 collective-permute-start.8
  875.0 1.9 collective-permute-start.7
  877.0 1.9 collective-permute-start.6
  878.9 4.3 collective-permute-start.5
  883.2 5.9 convolution_add_fusion.1
  891.0 8.9 collective-permute-start.4
  899.9 1.9 collective-permute-start.3
  901.9 4.6 collective-permute-start.2
  906.4 1.9 collective-permute-start.1
  908.4 1.9 collective-permute-start
  910.3 2.4 fusion.82
  913.4 1.8 collective-permute-done
  915.1 22.8 %concatenate.64 = f32[548,1024]{1,0:T(8,128)} concatenate(f32[28,1024]{1,0:T(8,128)} %collective-permute-done.12, f32[40,1024]{1,0:T(8,128)} %copy-done.59, f32[40,1024]{1,0:T(8,128)} %collective-permute-done.10, f32[40,1024]{1,0:T(8,128)} %collective-permute-done.9, f32[40,1024]{1,0:T(8,128)} %collective-permute-done.8, f32[40,1024]{1,0:T(8,128)} %collective-permute-done.7, ...), dimensions={0} | concatenate | bytes 4489216
  937.9 2.0 multiply_subtract_fusion.2
  941.0 3.9 fusion.92
  945.0 74.7 %all-reduce.2 = f32[2176]{0:T(1024)S(1)} all-reduce(f32[2176]{0:T(1024)S(1)} %concatenate.63), channel_id=8, replica_groups=mesh['rep'=16,'shard'=8] {'rep','shard'}, use_global_device_ids=true, to_apply=%region_31.32.clone | all-reduce | flops 2176 | bytes 17408
  1021.3 86.7 %reduce-scatter.14.cloned.1.call-done = f32[8,1024]{1,0:T(8,128)} async-done(((f32[1024,1024]{1,0:T(8,128)}), f32[8,1024]{1,0:T(8,128)}) %reduce-scatter.14.cloned.1.call-update) | async-done | bytes 32784 | tf_op jit(solution)/shard_map/reduce_scatter | solution.py:372
  1109.4 644.8 %reduce-scatter.12.cloned.1.call-done = f32[8,2048]{1,0:T(8,128)} async-done(((f32[1024,2048]{1,0:T(8,128)}), f32[8,2048]{1,0:T(8,128)}) %reduce-scatter.12.cloned.1.call-update) | async-done | bytes 65552 | tf_op jit(solution)/shard_map/reduce_scatter | solution.py:371
  1755.7 283.5 %reduce-scatter.16.cloned.1.call-done = f32[8,9216]{1,0:T(8,128)} async-done(((f32[1024,9216]{1,0:T(8,128)}), f32[8,9216]{1,0:T(8,128)}) %reduce-scatter.16.cloned.1.call-update) | async-done | bytes 294928 | tf_op jit(solution)/shard_map/reduce_scatter | solution.py:373
  2039.2 2.0 multiply_subtract_fusion
  (331 shorter events, 56.8 us)
Async XLA Ops:
  7.2 79.0 %copy-start.85 = (s32[1,3]{1,0:T(1,128)S(1)}, s32[1,3]{1,0:T(1,128)}, u32[]{:S(2)}) copy-start(s32[1,3]{1,0:T(1,128)} %param.26) | copy-start | bytes 40
  7.2 75.1 %all-gather.8.cloned.1.call-start = ((), (), s32[]{:S(2)}) async-start(), calls=%async_computation.5 | async-start | bytes 4227072 | tf_op jit(solution)/shard_map/all_gather | solution.py:221
  8.7 98.8 %all-gather.12.cloned.1.call-start = ((), (), s32[]{:S(2)}) async-start(), calls=%async_computation.7 | async-start | bytes 1179648 | tf_op jit(solution)/shard_map/all_gather | solution.py:268
  86.1 47.1 %all-gather.10.cloned.1.call-start = ((), (), s32[]{:S(2)}) async-start(), calls=%async_computation.6 | async-start | bytes 1179648 | tf_op jit(solution)/shard_map/all_gather | solution.py:267
  87.8 115.2 %all-gather.14.cloned.1.call-start = ((), (), s32[]{:S(2)}) async-start(), calls=%async_computation.8 | async-start | bytes 2113536 | tf_op jit(solution)/shard_map/all_gather | solution.py:222
  88.5 187.1 %all-gather.18.cloned.1.call-start = ((), (), s32[]{:S(2)}) async-start(), calls=%async_computation.14 | async-start | bytes 10567680 | tf_op jit(solution)/shard_map/all_gather | solution.py:224
  89.2 271.3 %all-gather.16.cloned.1.call-start = ((), (), s32[]{:S(2)}) async-start(), calls=%async_computation.9 | async-start | bytes 19021824 | tf_op jit(solution)/shard_map/all_gather | solution.py:223
  90.0 342.0 %reduce-scatter.18.cloned.1.call-start = ((), (), s32[]{:S(2)}) async-start(), calls=%async_computation.15 | async-start | bytes 1179648
  136.6 66.4 %copy-start.15 = (bf16[128,1024]{1,0:T(8,128)(2,1)S(1)}, bf16[128,1024]{1,0:T(8,128)(2,1)}, u32[]{:S(2)}) copy-start(bf16[128,1024]{1,0:T(8,128)(2,1)} %param.24) | copy-start | bytes 786436
  141.1 147.6 %copy-start.45 = (bf16[1024,8,64]{0,2,1:T(8,128)(2,1)}, bf16[1024,8,64]{0,2,1:T(8,128)(2,1)S(1)}, u32[]{:S(2)}) copy-start(bf16[1024,8,64]{0,2,1:T(8,128)(2,1)S(1)} %get-tuple-element.810) | copy-start | bytes 3145732
  141.1 147.6 %copy-start.61 = (s32[128]{0:T(128)}, s32[128]{0:T(128)S(1)}, u32[]{:S(2)}) copy-start(s32[128]{0:T(128)S(1)} %get-tuple-element.826) | copy-start | bytes 1540
  141.1 147.6 %copy-start.79 = (f32[8,2,128]{2,1,0:T(2,128)}, f32[8,2,128]{2,1,0:T(2,128)S(1)}, u32[]{:S(2)}) copy-start(f32[8,2,128]{2,1,0:T(2,128)S(1)} %get-tuple-element.834) | copy-start | bytes 24580
  141.2 147.6 %copy-start.28 = (bf16[8,2,128,64]{2,3,1,0:T(8,128)(2,1)}, bf16[8,2,128,64]{2,3,1,0:T(8,128)(2,1)S(1)}, u32[]{:S(2)}) copy-start(bf16[8,2,128,64]{2,3,1,0:T(8,128)(2,1)S(1)} %convert_element_type.116) | copy-start | bytes 786436
  205.1 181.4 %copy-start.5 = (f32[128,1024]{1,0:T(8,128)}, f32[128,1024]{1,0:T(8,128)S(1)}, u32[]{:S(2)}) copy-start(f32[128,1024]{1,0:T(8,128)S(1)} %get-tuple-element.425) | copy-start | bytes 1572868
  205.1 155.4 %copy-start.72 = (f32[128]{0:T(128)}, f32[128]{0:T(128)S(1)}, u32[]{:S(2)}) copy-start(f32[128]{0:T(128)S(1)} %add_rsqrt_fusion.2) | copy-start | bytes 1540
  398.3 66.8 %reduce-scatter.10.cloned.1.call-start = ((), (), s32[]{:S(2)}) async-start(), calls=%async_computation.10 | async-start | bytes 1179648 | tf_op jit(solution)/shard_map/reduce_scatter | solution.py:338
  401.7 706.2 %reduce-scatter.14.cloned.1.call-start = ((), (), s32[]{:S(2)}) async-start(), calls=%async_computation.12 | async-start | bytes 4227072 | tf_op jit(solution)/shard_map/reduce_scatter | solution.py:372
  404.5 1349.7 %reduce-scatter.12.cloned.1.call-start = ((), (), s32[]{:S(2)}) async-start(), calls=%async_computation.11 | async-start | bytes 8454144 | tf_op jit(solution)/shard_map/reduce_scatter | solution.py:371
  410.5 60.2 %copy-start.41 = (bf16[128,1024]{1,0:T(8,128)(2,1)}, bf16[128,1024]{1,0:T(8,128)(2,1)S(1)}, u32[]{:S(2)}) copy-start(bf16[128,1024]{1,0:T(8,128)(2,1)S(1)} %multiply_convert_fusion.3) | copy-start | bytes 786436
  470.7 1568.5 %reduce-scatter.16.cloned.1.call-start = ((), (), s32[]{:S(2)}) async-start(), calls=%async_computation.13 | async-start | bytes 38043648 | tf_op jit(solution)/shard_map/reduce_scatter | solution.py:373
  497.3 371.1 %copy-start.67 = (f32[128,8]{0,1:T(8,128)S(1)}, f32[128,8]{0,1:T(8,128)}, u32[]{:S(2)}) copy-start(f32[128,8]{0,1:T(8,128)} %copy-done.65) | copy-start | bytes 12292
  497.3 371.2 %copy-start.24 = (f32[128,512]{1,0:T(8,128)S(1)}, f32[128,512]{1,0:T(8,128)}, u32[]{:S(2)}) copy-start(f32[128,512]{1,0:T(8,128)} %copy-done.23) | copy-start | bytes 786436
  497.3 372.2 %copy-start.20 = (f32[128,1024]{1,0:T(8,128)S(1)}, f32[128,1024]{1,0:T(8,128)}, u32[]{:S(2)}) copy-start(f32[128,1024]{1,0:T(8,128)} %copy-done.19) | copy-start | bytes 1572868
  861.7 15.3 collective-permute-start.11
  863.0 15.9 collective-permute-start.10
  866.5 8.5 collective-permute-start.12
  871.0 20.0 collective-permute-start.9
  873.1 26.9 %collective-permute-start.8 = (f32[40,1024]{1,0:T(8,128)}, f32[40,1024]{1,0:T(8,128)}, u32[]{:S(2)}, u32[]{:S(2)}) collective-permute-start(f32[40,1024]{1,0:T(8,128)} %fusion.6), channel_id=1, source_target_pairs={{0,9},{1,10},{2,11},{3,12},{4,13},{5,14},{6,15},{7,16},{8,17},{9,1... | collective-permute-start | bytes 491528
  875.0 26.9 %collective-permute-start.7 = (f32[40,1024]{1,0:T(8,128)}, f32[40,1024]{1,0:T(8,128)}, u32[]{:S(2)}, u32[]{:S(2)}) collective-permute-start(f32[40,1024]{1,0:T(8,128)} %fusion.6), channel_id=1, source_target_pairs={{0,8},{1,9},{2,10},{3,11},{4,12},{5,13},{6,14},{7,15},{8,16},{9,17... | collective-permute-start | bytes 491528
  877.0 29.5 %collective-permute-start.6 = (f32[40,1024]{1,0:T(8,128)}, f32[40,1024]{1,0:T(8,128)}, u32[]{:S(2)}, u32[]{:S(2)}) collective-permute-start(f32[40,1024]{1,0:T(8,128)} %fusion.6), channel_id=1, source_target_pairs={{0,7},{1,8},{2,9},{3,10},{4,11},{5,12},{6,13},{7,14},{8,15},{9,16}... | collective-permute-start | bytes 491528
  878.9 29.5 %collective-permute-start.5 = (f32[40,1024]{1,0:T(8,128)}, f32[40,1024]{1,0:T(8,128)}, u32[]{:S(2)}, u32[]{:S(2)}) collective-permute-start(f32[40,1024]{1,0:T(8,128)} %fusion.6), channel_id=1, source_target_pairs={{0,6},{1,7},{2,8},{3,9},{4,10},{5,11},{6,12},{7,13},{8,14},{9,15},... | collective-permute-start | bytes 491528
  891.0 21.7 %collective-permute-start.4 = (f32[40,1024]{1,0:T(8,128)}, f32[40,1024]{1,0:T(8,128)}, u32[]{:S(2)}, u32[]{:S(2)}) collective-permute-start(f32[40,1024]{1,0:T(8,128)} %fusion.6), channel_id=1, source_target_pairs={{0,5},{1,6},{2,7},{3,8},{4,9},{5,10},{6,11},{7,12},{8,13},{9,14},{... | collective-permute-start | bytes 491528
  899.9 12.8 collective-permute-start.3
  901.9 10.9 collective-permute-start.2
  906.4 6.9 collective-permute-start.1
  908.4 6.7 collective-permute-start
  940.2 79.4 %copy-start.86 = (f32[17]{0:T(128)S(1)}, f32[17]{0:T(128)}, u32[]{:S(2)}) copy-start(f32[17]{0:T(128)} %param.31) | copy-start | bytes 208
  940.2 79.4 %copy-start.87 = (f32[17]{0:T(128)S(1)}, f32[17]{0:T(128)}, u32[]{:S(2)}) copy-start(f32[17]{0:T(128)} %param.36) | copy-start | bytes 208
  940.2 79.4 %copy-start.88 = (f32[17]{0:T(128)S(1)}, f32[17]{0:T(128)}, u32[]{:S(2)}) copy-start(f32[17]{0:T(128)} %param.41) | copy-start | bytes 208
  940.9 167.1 %copy-start.64 = (f32[8,1024]{1,0:T(8,128)S(1)}, f32[8,1024]{1,0:T(8,128)}, u32[]{:S(2)}) copy-start(f32[8,1024]{1,0:T(8,128)} %param.28) | copy-start | bytes 98308
  940.9 167.1 %copy-start.70 = (f32[8,1024]{1,0:T(8,128)S(1)}, f32[8,1024]{1,0:T(8,128)}, u32[]{:S(2)}) copy-start(f32[8,1024]{1,0:T(8,128)} %param.33) | copy-start | bytes 98308
  940.9 167.0 %copy-start.71 = (f32[8,1024]{1,0:T(8,128)S(1)}, f32[8,1024]{1,0:T(8,128)}, u32[]{:S(2)}) copy-start(f32[8,1024]{1,0:T(8,128)} %param.38) | copy-start | bytes 98308
  940.9 813.2 %copy-start.56 = (f32[8,2048]{1,0:T(8,128)S(1)}, f32[8,2048]{1,0:T(8,128)}, u32[]{:S(2)}) copy-start(f32[8,2048]{1,0:T(8,128)} %param.27) | copy-start | bytes 196612
  941.0 813.2 %copy-start.68 = (f32[8,2048]{1,0:T(8,128)S(1)}, f32[8,2048]{1,0:T(8,128)}, u32[]{:S(2)}) copy-start(f32[8,2048]{1,0:T(8,128)} %param.32) | copy-start | bytes 196612
  941.0 813.2 %copy-start.69 = (f32[8,2048]{1,0:T(8,128)S(1)}, f32[8,2048]{1,0:T(8,128)}, u32[]{:S(2)}) copy-start(f32[8,2048]{1,0:T(8,128)} %param.37) | copy-start | bytes 196612
  941.0 1098.2 %copy-start.38 = (f32[8,9216]{1,0:T(8,128)S(1)}, f32[8,9216]{1,0:T(8,128)}, u32[]{:S(2)}) copy-start(f32[8,9216]{1,0:T(8,128)} %param.29) | copy-start | bytes 884740
  941.0 1098.2 %copy-start.54 = (f32[8,9216]{1,0:T(8,128)S(1)}, f32[8,9216]{1,0:T(8,128)}, u32[]{:S(2)}) copy-start(f32[8,9216]{1,0:T(8,128)} %param.34) | copy-start | bytes 884740
  941.0 1098.2 %copy-start.55 = (f32[8,9216]{1,0:T(8,128)S(1)}, f32[8,9216]{1,0:T(8,128)}, u32[]{:S(2)}) copy-start(f32[8,9216]{1,0:T(8,128)} %param.39) | copy-start | bytes 884740
  (65 other events, 715.0 us)
Sparse Core Ops, SparseCore 0:
  11.8 70.4 all-gather.7
  86.2 21.1 all-gather.11
  109.7 23.4 all-gather.9
  136.8 66.1 all-gather.13
  206.5 69.0 all-gather.17
  279.1 81.4 all-gather.15
  398.4 33.4 reduce-scatter.17
  434.4 30.7 reduce-scatter.9
  467.5 640.4 reduce-scatter.13
  1110.3 643.8 reduce-scatter.11
  1759.7 279.5 reduce-scatter.15
where the time goes:
time: 2060 us; the launch traced here: 2050 us
  waiting for transfers between devices  1310 us (64%)
  blocking collectives  508 us (25%)
  matrix products  83.1 us (4%)
  local copies, waits for them, and re-layouts  62.4 us (3%)
  starting transfers between devices  37.3 us (2%)
  other arithmetic  26.4 us (1%)
    reduce_scatter x1, waiting for transfers between devices, local(): lax.psum_scatter(qkv_grad, ('rep', 'shard'), scatter_dimension=0, tiled=T...  645 us
    unnamed x3, blocking collectives  508 us
    reduce_scatter x1, waiting for transfers between devices, local(): lax.psum_scatter(gate_grad, ('rep', 'shard'), scatter_dimension=0, tiled=...  283 us
    reduce_scatter x1, waiting for transfers between devices, local(): lax.psum_scatter(out_grad, ('rep', 'shard'), scatter_dimension=0, tiled=T...  86.7 us
    all_gather x1, waiting for transfers between devices, local(): lax.all_gather(gate_low, ('rep', 'shard'), axis=0, tiled=True)  71.8 us
    all_gather x1, waiting for transfers between devices, local(): lax.all_gather(down_low, ('rep', 'shard'), axis=0, tiled=True)  70.5 us
    all_gather x1, waiting for transfers between devices, local(): lax.all_gather(out_low, ('rep', 'shard'), axis=0, tiled=True)  61.8 us
    unnamed x173, local copies, waits for them, and re-layouts  45.6 us
  transfers between devices with their start and end apart: 24, of which 13 were waited for; matrix products, arithmetic and copies ran while one was open for 24% of the time, Pallas kernels for 0%

commit v1 on v0

v1 whole, which is shorter than its diff:
```python
import jax
import jax.numpy as jnp
from jax import lax
from jax.experimental import pallas as pl
from jax.experimental.pallas import tpu as pltpu
from jax.sharding import PartitionSpec as P

D = 1024
FF = 4608
HEAD_SIZE = 64
STEP = 10
QUERY_FEATURES = 1024
KEY_FEATURES = 512
WO_FAN = 4

norm_eps = 1e-05
theta = 1000000.0
beta_one = 0.9
beta_two = 0.95
adam_eps = 1e-08
decay = 0.1
rate_scale = 2.0
gain_rate = 1.0
masked_score = -1e30

SHARDS = 8
CHIPS = 4
FF_OWN = FF // SHARDS
FF_PAD = 640
ROWS_FF_PAD = 40
QUERY_BLOCK = 256
score_scale = HEAD_SIZE ** (-0.5)
low = jnp.bfloat16
wide = jnp.float32
sibling = [(i, i ^ 1) for i in range(SHARDS)]


def from_chip(k):
    return [(i, ((i // 2 - k) % CHIPS) * 2 + i % 2) for i in range(SHARDS)]


def gather_rows(rows):
    parts = [rows] + [lax.ppermute(rows, "shard", from_chip(k)) for k in range(1, CHIPS)]
    mine = jnp.concatenate(parts, axis=0)
    other = lax.ppermute(mine, "shard", sibling)
    return jnp.concatenate([mine, other], axis=0)


def scatter_rows(mine, other):
    count = mine.shape[0] // CHIPS
    got = lax.ppermute(other.astype(low), "shard", sibling)
    both = mine + got.astype(wide)
    sent = both.astype(low)
    total = both[:count]
    for k in (2, 1, 3):
        total = total + lax.ppermute(
            sent[k * count : (k + 1) * count], "shard", from_chip(-k)
        ).astype(wide)
    return total


def norm_pieces(field):
    scale = lax.rsqrt(jnp.mean(field * field, axis=-1, keepdims=True) + norm_eps)
    return field * scale, scale


def norm_back(incoming_grad, normed, scale, gain):
    gain_grad = jnp.sum(incoming_grad * normed, axis=0)
    scaled = incoming_grad * gain
    inner = jnp.mean(scaled * normed, axis=-1, keepdims=True)
    return gain_grad, scale * (scaled - normed * inner)


def sequence_info(lengths_row, index):
    ends = jnp.cumsum(lengths_row)
    passed = ends[None, :] <= index[:, None]
    return jnp.sum(jnp.where(passed, lengths_row[None, :], 0), axis=1)


def rotation_tables(places):
    half = HEAD_SIZE // 2
    freqs = theta ** (-(jnp.arange(half, dtype=wide) * 2.0) / HEAD_SIZE)
    angles = places.astype(wide)[:, None] * freqs[None, :]
    cos, sin = jnp.cos(angles), jnp.sin(angles)
    return jnp.concatenate([cos] * 4, axis=1), jnp.concatenate([-sin, sin, -sin, sin], axis=1)


def lanes(rows):
    return lax.broadcasted_iota(jnp.int32, (rows, 2 * HEAD_SIZE), 1)


def partner(field):
    first = lanes(field.shape[0]) % HEAD_SIZE < HEAD_SIZE // 2
    return jnp.where(first, pltpu.roll(field, 96, 1), pltpu.roll(field, 32, 1))


def left_mean(field):
    left = lanes(field.shape[0]) < HEAD_SIZE
    return jnp.sum(jnp.where(left, field, 0.0), axis=1, keepdims=True) / HEAD_SIZE


def head_means(field):
    left = lanes(field.shape[0]) < HEAD_SIZE
    one = jnp.sum(jnp.where(left, field, 0.0), axis=1, keepdims=True) / HEAD_SIZE
    two = jnp.sum(jnp.where(left, 0.0, field), axis=1, keepdims=True) / HEAD_SIZE
    return jnp.where(left, one, two)


def swap_heads(field):
    return pltpu.roll(field, HEAD_SIZE, 1)


def stack_heads(block):
    left = (lax.broadcasted_iota(jnp.int32, (1, 2 * HEAD_SIZE), 1) < HEAD_SIZE).astype(wide)
    return jnp.concatenate([block * left.astype(low), block * (1.0 - left).astype(low)], axis=0)


def allowed_keys(start_ref, block, keys):
    begin = start_ref[block * QUERY_BLOCK : (block + 1) * QUERY_BLOCK, :]
    begin = jnp.concatenate([begin, begin], axis=0)
    row = lax.broadcasted_iota(jnp.int32, (2 * QUERY_BLOCK, keys), 0)
    row = block * QUERY_BLOCK + jnp.where(row >= QUERY_BLOCK, row - QUERY_BLOCK, row)
    col = lax.broadcasted_iota(jnp.int32, (2 * QUERY_BLOCK, keys), 1)
    return (col >= begin) & (col <= row)


def dot_last(one, two):
    return lax.dot_general(one, two, (((1,), (1,)), ((), ())), preferred_element_type=wide)


def dot_first(one, two):
    return lax.dot_general(one, two, (((0,), (0,)), ((), ())), preferred_element_type=wide)


def forward_kernel(
    place_ref, proj_ref, cos_ref, sin_ref, start_ref, gain_ref,
    out_ref, query_ref, key_ref, value_ref, shift_ref, mixed_ref,
):
    count = proj_ref.shape[0] // SHARDS
    left = lanes(count) < HEAD_SIZE
    gain_query = gain_ref[:, :128]
    gain_key = gain_ref[:, 128:]
    for chunk in range(SHARDS):
        place = pl.multiple_of(place_ref[chunk], 128)
        rows = slice(chunk * count, (chunk + 1) * count)
        there = pl.ds(place, count)
        cos, sin = cos_ref[there, :], sin_ref[there, :]
        query = proj_ref[rows, :128]
        query = query * lax.rsqrt(head_means(query * query) + norm_eps) * gain_query
        query = (query * cos + partner(query) * sin).astype(low)
        query_ref[there, :] = query * jnp.asarray(score_scale, low)
        both = proj_ref[rows, 128:]
        key = both * lax.rsqrt(left_mean(both * both) + norm_eps) * gain_key
        key = key * cos + partner(key) * sin
        both = jnp.where(left, key, both)
        turned = swap_heads(both)
        key_ref[there, :] = jnp.where(left, both, turned).astype(low)
        value_ref[there, :] = jnp.where(left, turned, both).astype(low)
    half = lanes(QUERY_BLOCK) < HEAD_SIZE
    for block in range(proj_ref.shape[0] // QUERY_BLOCK):
        keys = (block + 1) * QUERY_BLOCK
        span = slice(block * QUERY_BLOCK, keys)
        query = stack_heads(query_ref[span, :])
        raw = dot_last(query, key_ref[:keys, :])
        raw = jnp.where(allowed_keys(start_ref, block, keys), raw, masked_score)
        top = jnp.max(raw, axis=1, keepdims=True)
        weight = jnp.exp(raw - top)
        total = jnp.sum(weight, axis=1, keepdims=True)
        probs = (weight * (1.0 / total)).astype(low)
        mixed = jnp.dot(probs, value_ref[:keys, :], preferred_element_type=wide)
        mixed_ref[span, :] = jnp.where(half, mixed[:QUERY_BLOCK], mixed[QUERY_BLOCK:])
        shift_ref[2 * block * QUERY_BLOCK : 2 * keys, :] = top + jnp.log(total)
    for chunk in range(SHARDS):
        place = pl.multiple_of(place_ref[chunk], 128)
        out_ref[chunk * count : (chunk + 1) * count, :] = mixed_ref[pl.ds(place, count), :].astype(low)


def backward_kernel(
    place_ref, proj_ref, cos_ref, sin_ref, start_ref, gain_ref, query_ref, key_ref, value_ref,
    shift_ref, incoming_ref, out_ref, gain_grad_ref, back_ref, query_grad_ref, key_grad_ref,
    value_grad_ref,
):
    count = proj_ref.shape[0] // SHARDS
    left = lanes(count) < HEAD_SIZE
    gain_query = gain_ref[:, :128]
    gain_key = gain_ref[:, 128:]
    for chunk in range(SHARDS):
        place = pl.multiple_of(place_ref[chunk], 128)
        back_ref[pl.ds(place, count), :] = incoming_ref[chunk * count : (chunk + 1) * count, :]
    key_grad_ref[...] = jnp.zeros_like(key_grad_ref)
    value_grad_ref[...] = jnp.zeros_like(value_grad_ref)
    half = lanes(QUERY_BLOCK) < HEAD_SIZE
    for block in range(proj_ref.shape[0] // QUERY_BLOCK):
        keys = (block + 1) * QUERY_BLOCK
        span = slice(block * QUERY_BLOCK, keys)
        query = stack_heads(query_ref[span, :])
        back = stack_heads(back_ref[span, :])
        raw = dot_last(query, key_ref[:keys, :])
        shift = shift_ref[2 * block * QUERY_BLOCK : 2 * keys, :]
        probs = jnp.where(allowed_keys(start_ref, block, keys), jnp.exp(raw - shift), 0.0)
        prob_grad = dot_last(back, value_ref[:keys, :])
        spread = jnp.sum(probs * prob_grad, axis=1, keepdims=True)
        score_grad = (probs * (prob_grad - spread)).astype(low)
        query_grad = jnp.dot(score_grad, key_ref[:keys, :], preferred_element_type=wide)
        query_grad_ref[span, :] = score_scale * jnp.where(
            half, query_grad[:QUERY_BLOCK], query_grad[QUERY_BLOCK:]
        )
        key_grad_ref[:keys, :] += dot_first(score_grad, query)
        value_grad_ref[:keys, :] += dot_first(probs.astype(low), back)
    gain_query_grad = jnp.zeros((1, 128), wide)
    gain_key_grad = jnp.zeros((1, 128), wide)
    for chunk in range(SHARDS):
        place = pl.multiple_of(place_ref[chunk], 128)
        rows = slice(chunk * count, (chunk + 1) * count)
        there = pl.ds(place, count)
        cos, sin = cos_ref[there, :], sin_ref[there, :]
        query = proj_ref[rows, :128]
        scale = lax.rsqrt(head_means(query * query) + norm_eps)
        query = query * scale
        grad = query_grad_ref[there, :]
        grad = grad * cos - partner(grad) * sin
        gain_query_grad += jnp.sum(grad * query, axis=0, keepdims=True)
        grad = grad * gain_query
        out_ref[rows, :128] = (scale * (grad - query * head_means(grad * query))).astype(low)
        key = proj_ref[rows, 128:]
        scale = lax.rsqrt(left_mean(key * key) + norm_eps)
        key = key * scale
        grad = key_grad_ref[there, :]
        grad = grad + swap_heads(grad)
        grad = grad * cos - partner(grad) * sin
        gain_key_grad += jnp.sum(grad * key, axis=0, keepdims=True)
        grad = grad * gain_key
        grad = scale * (grad - key * left_mean(grad * key))
        value_grad = value_grad_ref[there, :]
        value_grad = value_grad + swap_heads(value_grad)
        out_ref[rows, 128:] = jnp.where(left, grad, value_grad).astype(low)
    gain_grad_ref[:, :128] = gain_query_grad
    gain_grad_ref[:, 128:] = gain_key_grad


def in_vmem(count):
    return [pl.BlockSpec(memory_space=pltpu.VMEM)] * count


def attention_forward(place, projected, cos, sin, start, gain):
    rows = projected.shape[0]
    return pl.pallas_call(
        forward_kernel,
        out_shape=[jax.ShapeDtypeStruct((rows, 128), low)] * 4
        + [jax.ShapeDtypeStruct((2 * rows, 1), wide)],
        in_specs=[pl.BlockSpec(memory_space=pltpu.SMEM)] + in_vmem(5),
        out_specs=in_vmem(5),
        scratch_shapes=[pltpu.VMEM((rows, 128), wide)],
        compiler_params=pltpu.CompilerParams(vmem_limit_bytes=40 * 2**20),
        cost_estimate=pl.CostEstimate(
            flops=10**9, bytes_accessed=5 * 2**20, transcendentals=2 * 10**6
        ),
        name="attention_forward",
    )(place, projected, cos, sin, start, gain)


def attention_backward(place, projected, cos, sin, start, gain, query, key, value, shift, incoming):
    rows = projected.shape[0]
    return pl.pallas_call(
        backward_kernel,
        out_shape=[
            jax.ShapeDtypeStruct((rows, 256), low),
            jax.ShapeDtypeStruct((1, 256), wide),
        ],
        in_specs=[pl.BlockSpec(memory_space=pltpu.SMEM)] + in_vmem(10),
        out_specs=in_vmem(2),
        scratch_shapes=[pltpu.VMEM((rows, 128), low)] + [pltpu.VMEM((rows, 128), wide)] * 3,
        compiler_params=pltpu.CompilerParams(vmem_limit_bytes=48 * 2**20),
        cost_estimate=pl.CostEstimate(
            flops=3 * 10**9, bytes_accessed=6 * 2**20, transcendentals=2 * 10**6
        ),
        name="attention_backward",
    )(place, projected, cos, sin, start, gain, query, key, value, shift, incoming)


def adamw(weight, grad, first, second, rate, weight_decay):
    new_first = beta_one * first + (1.0 - beta_one) * grad
    new_second = beta_two * second + (1.0 - beta_two) * grad * grad
    step_size = (
        new_first
        / (1.0 - beta_one**STEP)
        / (jnp.sqrt(new_second / (1.0 - beta_two**STEP)) + adam_eps)
    )
    return (weight - rate * (step_size + weight_decay * weight), new_first, new_second)


def fold(field):
    width = field.shape[-1]
    return jnp.concatenate([field[..., i : i + 256] for i in range(0, width, 256)], axis=-2)


def unfold(field, width):
    count = width // 256
    rows = field.shape[-2] // count
    return jnp.concatenate([field[..., i * rows : (i + 1) * rows, :] for i in range(count)], axis=-1)


def pad_to(field, size, axis):
    widths = [(0, 0)] * field.ndim
    widths[axis] = (0, size - field.shape[axis])
    return jnp.pad(field, widths)


def dot(one, two):
    return jnp.dot(one, two, preferred_element_type=wide)


def dot_back(one, two):
    return jnp.einsum("tc,dc->td", one, two, preferred_element_type=wide)


def dot_rows(one, two):
    return jnp.einsum("td,tc->dc", one, two, preferred_element_type=wide)


def local(
    tokens, cotangent, lengths,
    qkv_proj, out_proj, gate_proj, down_proj, norm_gains,
    qkv_first, out_first, gate_first, down_first, gain_first,
    qkv_second, out_second, gate_second, down_second, gain_second,
):
    reps = lax.axis_size("rep")
    rows = tokens.shape[0]
    half = rows * SHARDS // 2
    own = qkv_proj.shape[0]
    block = own * SHARDS
    own_gains = norm_gains.shape[0]
    own_out = out_proj.shape[0]
    own_down = down_proj.shape[0]
    both_axes = ("rep", "shard")
    to_group = [(s * reps + r, r * SHARDS + s) for r in range(reps) for s in range(SHARDS)]
    to_owner = [(b, a) for a, b in to_group]

    token_rows = gather_rows(tokens)
    qkv_low = qkv_proj.astype(low)
    qkv_out = jnp.stack(
        [
            jnp.concatenate(
                [
                    qkv_low[:, 128 * s : 128 * s + 128],
                    qkv_low[:, QUERY_FEATURES + 64 * s : QUERY_FEATURES + 64 * s + 64],
                    qkv_low[
                        :,
                        QUERY_FEATURES + KEY_FEATURES + 64 * s : QUERY_FEATURES
                        + KEY_FEATURES
                        + 64 * s
                        + 64,
                    ],
                ],
                axis=1,
            )
            for s in range(SHARDS)
        ]
    )
    gate_low = gate_proj.astype(low)
    gate_out = jnp.stack(
        [
            jnp.concatenate(
                [
                    pad_to(gate_low[:, FF_OWN * s : FF_OWN * (s + 1)], FF_PAD, 1),
                    pad_to(gate_low[:, FF + FF_OWN * s : FF + FF_OWN * (s + 1)], FF_PAD, 1),
                ],
                axis=1,
            )
            for s in range(SHARDS)
        ]
    )
    gain_lanes = -(-own_gains // 128) * 128
    gain_out = jnp.broadcast_to(
        pad_to(pad_to(norm_gains.astype(low)[None, :], gain_lanes, 1), own, 0)[None],
        (SHARDS, own, gain_lanes),
    )
    turned = lax.all_to_all(
        jnp.concatenate([qkv_out, gate_out, gain_out], axis=2), "shard", 0, 0, tiled=True
    )
    down_pad = pad_to(down_proj.astype(low), ROWS_FF_PAD * (own_down // 36), 0)
    moved = lax.ppermute(
        jnp.concatenate([out_proj.astype(low), down_pad], axis=0), both_axes, to_group
    )
    first_parts = jnp.concatenate(
        [
            turned[:, :, :256].reshape(block, 256),
            fold(moved[:own_out]),
            pad_to(turned[:, 0, 1536:], 256, 1),
        ],
        axis=0,
    )
    second_parts = jnp.concatenate(
        [fold(turned[:, :, 256:1536].reshape(block, 2 * FF_PAD)), fold(moved[own_out:])], axis=0
    )
    first_all = lax.all_gather(first_parts, "rep", axis=0)
    second_all = lax.all_gather(second_parts, "rep", axis=0)
    qkv_w = first_all[:, :block].reshape(D, 256)
    out_w = unfold(first_all[:, block : block + 4 * own_out], D).reshape(reps * own_out, D)
    gains = first_all[:, block + 4 * own_out :, :own_gains].reshape(-1).astype(wide)
    gate_w = unfold(second_all[:, : 5 * block], 2 * FF_PAD).reshape(D, 2 * FF_PAD)
    down_w = unfold(second_all[:, 5 * block :], D)[:, :own_down].reshape(FF_OWN, D)
    down_w = pad_to(down_w, FF_PAD, 0)
    gain_attn = gains[:D]
    gain_query = gains[D : D + HEAD_SIZE]
    gain_key = gains[D + HEAD_SIZE : D + 2 * HEAD_SIZE]
    gain_ffn = gains[D + 2 * HEAD_SIZE :]
    gain_heads = jnp.concatenate([gain_query, gain_query, gain_key, gain_key])[None, :]

    shard_pos = lax.axis_index("shard")
    chip, core = shard_pos // 2, shard_pos % 2
    order = jnp.arange(SHARDS, dtype=jnp.int32)
    place = rows * (2 * ((chip + order % CHIPS) % CHIPS) + (core + order // CHIPS) % 2)
    place = place.astype(jnp.int32)
    index = jnp.arange(rows * SHARDS, dtype=jnp.int32)
    start = sequence_info(lengths[0], index)
    cos, sin = rotation_tables(index - start)
    start = start[:, None]

    inputs_all = token_rows.astype(wide)
    normed = (norm_pieces(inputs_all)[0] * gain_attn).astype(low)
    projected = dot(normed, qkv_w)
    mixed, query, key, value, shift = attention_forward(
        place, projected, cos, sin, start, gain_heads
    )
    inputs = tokens.astype(wide)
    residual = inputs + scatter_rows(dot(mixed[:half], out_w), dot(mixed[half:], out_w))
    residual_hat, residual_scale = norm_pieces(residual)
    normed_two = gather_rows((residual_hat * gain_ffn).astype(low))
    cotangent_rows = gather_rows(cotangent)
    hidden_grad = dot_back(cotangent_rows, down_w)
    both = dot(normed_two, gate_w)
    gate, upper = both[:, :FF_PAD], both[:, FF_PAD:]
    sigmoid_gate = jax.nn.sigmoid(gate)
    activated = gate * sigmoid_gate
    hidden = (activated * upper).astype(low)
    both_grad = jnp.concatenate(
        [
            hidden_grad * upper * sigmoid_gate * (1.0 + gate * (1.0 - sigmoid_gate)),
            hidden_grad * activated,
        ],
        axis=1,
    ).astype(low)

    normed_two_grad = scatter_rows(
        dot_back(both_grad[:half], gate_w), dot_back(both_grad[half:], gate_w)
    )
    gain_ffn_grad, residual_part = norm_back(
        normed_two_grad, residual_hat, residual_scale, gain_ffn
    )
    residual_grad = cotangent.astype(wide) + residual_part
    branch_grad = gather_rows(residual_grad.astype(low))
    block_output = residual + scatter_rows(dot(hidden[:half], down_w), dot(hidden[half:], down_w))
    gate_grad = dot_rows(normed_two, both_grad).astype(low)
    down_grad = dot_rows(hidden, cotangent_rows)[:FF_OWN].astype(low)
    ffn_grads = jnp.concatenate(
        [
            fold(gate_grad.reshape(reps, block, 2 * FF_PAD)),
            fold(pad_to(down_grad.reshape(reps, own_down, D), down_pad.shape[0], 1)),
        ],
        axis=1,
    )
    ffn_sums = lax.psum_scatter(
        ffn_grads.reshape(-1, 256), "rep", scatter_dimension=0, tiled=True
    )

    incoming = dot_back(branch_grad, out_w).astype(low)
    projected_grad, head_gain_grad = attention_backward(
        place, projected, cos, sin, start, gain_heads, query, key, value, shift, incoming
    )
    out_grad = dot_rows(mixed, branch_grad).astype(low)
    qkv_grad = dot_rows(normed, projected_grad).astype(low)
    last_grads = jnp.concatenate(
        [qkv_grad.reshape(reps, block, 256), fold(out_grad.reshape(reps, own_out, D))], axis=1
    )
    last_sums = jnp.sum(
        lax.all_to_all(last_grads, "rep", 0, 0, tiled=True).astype(wide), axis=0
    )
    normed_grad = scatter_rows(
        dot_back(projected_grad[:half], qkv_w), dot_back(projected_grad[half:], qkv_w)
    )
    input_hat, input_scale = norm_pieces(inputs)
    gain_attn_grad, input_part = norm_back(normed_grad, input_hat, input_scale, gain_attn)
    input_grad = residual_grad + input_part

    heads = head_gain_grad[0]
    gain_grad = jnp.concatenate(
        [
            gain_attn_grad,
            heads[:HEAD_SIZE] + heads[HEAD_SIZE : 2 * HEAD_SIZE],
            heads[2 * HEAD_SIZE : 3 * HEAD_SIZE],
            gain_ffn_grad,
        ]
    ).reshape(reps, 1, SHARDS * own_gains)
    gain_sums = jnp.sum(lax.all_to_all(gain_grad, "rep", 0, 0, tiled=True), axis=0)
    gain_back = pad_to(gain_sums.reshape(SHARDS, 1, own_gains), 256, 2)
    last_back = lax.all_to_all(
        jnp.concatenate([last_sums[:block].reshape(SHARDS, own, 256), gain_back], axis=1),
        "shard", 0, 0, tiled=True,
    )
    gain_total = jnp.sum(last_back[:, own, :own_gains], axis=0)
    qkv_total = jnp.concatenate(
        [last_back[s, :own, :128] for s in range(SHARDS)]
        + [last_back[s, :own, 128:192] for s in range(SHARDS)]
        + [last_back[s, :own, 192:] for s in range(SHARDS)],
        axis=1,
    )
    out_total = lax.ppermute(unfold(last_sums[block:], D), both_axes, to_owner)
    down_total = lax.ppermute(
        unfold(ffn_sums[5 * block :], D)[:own_down], both_axes, to_owner
    ).astype(wide)
    gate_back = lax.all_to_all(
        unfold(ffn_sums[: 5 * block], 2 * FF_PAD).reshape(SHARDS, own, 2 * FF_PAD),
        "shard", 0, 0, tiled=True,
    ).astype(wide)
    gate_total = jnp.concatenate(
        [gate_back[s, :, :FF_OWN] for s in range(SHARDS)]
        + [gate_back[s, :, FF_PAD : FF_PAD + FF_OWN] for s in range(SHARDS)],
        axis=1,
    )
    results = []
    for weight, grad, first, second, rate, weight_decay in (
        (qkv_proj, qkv_total, qkv_first, qkv_second, rate_scale * D ** (-0.5), decay),
        (out_proj, out_total, out_first, out_second, rate_scale * WO_FAN ** (-0.5), decay),
        (gate_proj, gate_total, gate_first, gate_second, rate_scale * D ** (-0.5), decay),
        (down_proj, down_total, down_first, down_second, rate_scale * FF ** (-0.5), decay),
        (norm_gains, gain_total, gain_first, gain_second, gain_rate, 0.0),
    ):
        results.extend(adamw(weight, grad, first, second, rate, weight_decay))
    return (block_output, input_grad, *results)


def solution(mesh):
    by_rows = P(("rep", "shard"), None)
    by_entry = P(("rep", "shard"))
    return jax.shard_map(
        local,
        mesh=mesh,
        in_specs=(by_rows, by_rows, P("rep", None)) + ((by_rows,) * 4 + (by_entry,)) * 3,
        out_specs=(by_rows,) * 14 + (by_entry,) * 3,
        check_vma=False,
    )
```

time: 2060 us -> 330 us (0.16)
  waiting for transfers between devices: 1310 us -> 75.2 us
  blocking collectives: 508 us -> 19.8 us
  matrix products: 83.1 us -> 31.7 us
  starting transfers between devices: 37.3 us -> 84.3 us
    reduce_scatter x4 -> x1, waiting for transfers between devices: 1040 us -> 0.01 us  [local(): lax.psum_scatter(ffn_grads.reshape(-1, 256), 'rep', scatter_dimension=0,...]
    unnamed x3 -> x0, blocking collectives: 508 us -> none
    all_gather x6 -> x1, waiting for transfers between devices: 247 us -> 0.01 us  [local(): second_all = lax.all_gather(second_parts, 'rep', axis=0)]
    ppermute x0 -> x35, starting transfers between devices: none -> 57.1 us  [the longest x12 16.3 us: gather_rows(): lax.ppermute(rows, 'shard', from_chip(k))]
    ppermute x0 -> x35, waiting for transfers between devices: none -> 52.8 us  [the longest x12 28.9 us: scatter_rows(): lax.ppermute(sent[k * count:(k + 1) * count], 'shard', from_chip(-k))]
    dot_general x21 -> x16, matrix products: 83.1 us -> 31.7 us  [the longest x6 14.3 us: dot(): return jnp.dot(one, two, preferred_element_type=wide)]
    unnamed x14 -> x0, starting transfers between devices: 36.7 us -> none
    all_to_all x0 -> x5, starting transfers between devices: none -> 27.1 us  [the longest x1 6.88 us: local(): lax.all_to_all(jnp.concatenate([qkv_out, gate_out, gain_out], axis=2), 's...]
  transfers between devices with their start and end apart: 24 -> 42, of which waited for: 13 -> 20; matrix products, arithmetic and copies ran while one was open for 24% -> 25% of each run, Pallas kernels for 0% -> 4%
where the time goes in v1:
time: 330 us; the launch traced here: 323 us
  starting transfers between devices  84.3 us (26%)
  waiting for transfers between devices  75.2 us (23%)
  local copies, waits for them, and re-layouts  53.1 us (16%)
  matrix products  31.7 us (10%)
  other arithmetic  30.9 us (9%)
  blocking collectives  19.8 us (6%)
  between operations  15.8 us (5%)
  Pallas kernels  12.6 us (4%)
    unnamed x164, local copies, waits for them, and re-layouts  33.3 us
    ppermute x12, waiting for transfers between devices, scatter_rows(): lax.ppermute(sent[k * count:(k + 1) * count], 'shard', from_chip(-k))  28.9 us
    ppermute x12, waiting for transfers between devices, gather_rows(): lax.ppermute(rows, 'shard', from_chip(k))  23.9 us
    all_gather x1, blocking collectives, local(): first_all = lax.all_gather(first_parts, 'rep', axis=0)  19.8 us
    ppermute x12, starting transfers between devices, gather_rows(): lax.ppermute(rows, 'shard', from_chip(k))  16.3 us
    dot_general x6, matrix products, dot(): return jnp.dot(one, two, preferred_element_type=wide)  14.3 us
    ppermute x12, starting transfers between devices, scatter_rows(): lax.ppermute(sent[k * count:(k + 1) * count], 'shard', from_chip(-k))  14 us
    ppermute x4, starting transfers between devices, gather_rows(): other = lax.ppermute(mine, 'shard', sibling)  12 us
  transfers between devices with their start and end apart: 42, of which 20 were waited for; matrix products, arithmetic and copies ran while one was open for 25% of the time, Pallas kernels for 4%

profile of v1, /device:TPU:1, one launch (start us, length us, event | category | flops | bytes accessed | tf_op | source)
XLA Modules:
  0.0 323.2 jit_solution(2183506338724944591)
XLA Ops:
  7.2 2.5 collective-permute-start.2
  9.7 3.3 %collective-permute-start.1 = (bf16[128,1024]{1,0:T(8,128)(2,1)}, bf16[128,1024]{1,0:T(8,128)(2,1)}, u32[]{:S(2)}, u32[]{:S(2)}) collective-permute-start(bf16[128,1024]{1,0:T(8,128)(2,1)} %param.18), channel_id=1, source_target_pairs={{0,4},{1,5},{2,6},{3,7},{4,0},{5,1},{6,2},{7,3},{8,12},{9,13},{10,... | collective-permute-start | bytes 786440 | tf_op jit(solution)/shard_map/ppermute | solution.py:43
  16.1 4.6 %collective-permute-start.4 = (bf16[48,1024]{1,0:T(8,128)(2,1)}, bf16[48,1024]{1,0:T(8,128)(2,1)S(1)}, u32[]{:S(2)}, u32[]{:S(2)}) collective-permute-start(bf16[48,1024]{1,0:T(8,128)(2,1)} %fusion.61), channel_id=1, source_target_pairs={{0,0},{16,1},{32,2},{48,3},{64,4},{80,5},{96,6},{112,7},{1,8},{17,... | collective-permute-start | bytes 294920 | tf_op jit(solution)/shard_map/ppermute | solution.py:382
  25.5 6.9 %all-to-all-start = ((bf16[8,8,1664]{2,1,0:T(8,128)(2,1)}), bf16[8,8,1664]{2,1,0:T(8,128)(2,1)}, u32[]{:S(2)}, u32[]{:S(2)}) async-start(bf16[8,8,1664]{2,1,0:T(8,128)(2,1)} %pad_maximum_fusion.11), calls=%async_computation | async-start | bytes 425984 | tf_op jit(solution)/shard_map/all_to_all | solution.py:378
  36.5 2.1 all-to-all-done
  41.9 19.8 %all-gather = bf16[1664,256]{1,0:T(8,128)(2,1)S(1)} all-gather(bf16[104,256]{1,0:T(8,128)(2,1)S(1)} %constant_dynamic-update-slice_fusion.21), channel_id=2, replica_groups=mesh['rep'=16,'shard'=8] {'rep'}, dimensions={0}, use_global_device_ids=true | all-gather | bytes 905216 | tf_op jit(solution)/shard_map/all_gather | solution.py:396
  63.4 6.0 %collective-permute-start.3 = (bf16[512,1024]{1,0:T(8,128)(2,1)S(1)}, bf16[512,1024]{1,0:T(8,128)(2,1)S(1)}, u32[]{:S(2)}, u32[]{:S(2)}) collective-permute-start(bf16[512,1024]{1,0:T(8,128)(2,1)S(1)} %pad_maximum_fusion.5), channel_id=1, source_target_pairs={{0,1},{1,0},{2,3},{3,2},{4,5},{5,4},{6,7},{7,6},{8,9},{9,8},{10,11... | collective-permute-start | bytes 3145736 | tf_op jit(solution)/shard_map/ppermute | solution.py:45
  73.9 5.8 %attention_forward.1 = (bf16[1024,128]{1,0:T(8,128)(2,1)S(1)}, bf16[1024,128]{1,0:T(8,128)(2,1)S(1)}, bf16[1024,128]{1,0:T(8,128)(2,1)S(1)}, bf16[1024,128]{1,0:T(8,128)(2,1)S(1)}, f32[2048,1]{1,0:T(8,128)S(1)}) custom-call(s32[8]{0:T(128)S(1)} %fusion.102.place_ref, f32[1024,256]{1,0:T(8,128)S(1)} %fusion.25.proj_ref, ...), custom_call_target="tpu_custom_call" | custom-call | flops 1000000000 | bytes 5242880 | tf_op jit(solution)/shard_map/attention_forward/pallas_call | solution.py:247
  80.5 2.5 collective-permute-start.18
  83.7 2.3 collective-permute-start.6
  89.0 5.6 %collective-permute-done.18 = bf16[128,1024]{1,0:T(8,128)(2,1)S(1)} collective-permute-done((bf16[128,1024]{1,0:T(8,128)(2,1)S(1)}, bf16[128,1024]{1,0:T(8,128)(2,1)S(1)}, u32[]{:S(2)}, u32[]{:S(2)}) %collective-permute-start.18) | collective-permute-done | bytes 262176 | tf_op jit(solution)/shard_map/ppermute | solution.py:43
  95.1 2.8 collective-permute-start.20
  97.8 2.5 collective-permute-done.6
  100.3 6.0 %collective-permute-done.8 = bf16[128,1024]{1,0:T(8,128)(2,1)S(1)} collective-permute-done((bf16[128,1024]{1,0:T(8,128)(2,1)S(1)}, bf16[128,1024]{1,0:T(8,128)(2,1)S(1)}, u32[]{:S(2)}, u32[]{:S(2)}) %collective-permute-start.8) | collective-permute-done | bytes 262176 | tf_op jit(solution)/shard_map/ppermute | solution.py:56
  109.0 3.1 collective-permute-start.10
  112.2 4.0 %collective-permute-done.11 = bf16[128,1024]{1,0:T(8,128)(2,1)S(1)} collective-permute-done((bf16[128,1024]{1,0:T(8,128)(2,1)S(1)}, bf16[128,1024]{1,0:T(8,128)(2,1)S(1)}, u32[]{:S(2)}, u32[]{:S(2)}) %collective-permute-start.11) | collective-permute-done | bytes 262176 | tf_op jit(solution)/shard_map/ppermute | solution.py:43
  116.2 7.4 %collective-permute-done.10 = bf16[128,1024]{1,0:T(8,128)(2,1)S(1)} collective-permute-done((bf16[128,1024]{1,0:T(8,128)(2,1)S(1)}, bf16[128,1024]{1,0:T(8,128)(2,1)S(1)}, u32[]{:S(2)}, u32[]{:S(2)}) %collective-permute-start.10) | collective-permute-done | bytes 262176 | tf_op jit(solution)/shard_map/ppermute | solution.py:43
  130.3 2.0 slice_dynamic-update-slice_fusion.9
  133.5 2.2 reshape.168
  135.7 2.0 slice_dynamic-update-slice_fusion.8
  137.7 1.9 slice_dynamic-update-slice_fusion.7
  141.5 1.9 slice_dynamic-update-slice_fusion.5
  143.4 5.4 %fusion.136 = f32[1024,1280]{1,0:T(8,128)S(1)} fusion(bf16[1024,1024]{1,0:T(8,128)(2,1)} %constant_dynamic-update-slice_fusion.27, bf16[1024,1280]{1,0:T(8,128)(2,1)} %bitcast.218), kind=kOutput, calls=%fused_computation.342 | convolution fusion | flops 2684354560 | bytes 9961472 | tf_op jit(solution)/shard_map/dot_general | solution.py:310
  148.9 2.8 multiply_convert_fusion
  153.6 4.5 %convolution_convert_fusion = bf16[1024,1280]{1,0:T(8,128)(2,1)S(1)} fusion(bf16[1024,1024]{1,0:T(8,128)(2,1)} %constant_dynamic-update-slice_fusion.27, bf16[1024,640]{1,0:T(8,128)(2,1)S(1)} %get-tuple-element.58, bf16[1024,640]{1,0:T(8,128)(2,1)S(1)} %get-tuple-element.59), kind=kOutput, calls=%fused_computation.5 | convolution fusion | flops 2690908160 | bytes 7340032 | tf_op jit(solution)/shard_map/td,tc->dc/dot_general | solution.py:318
  167.4 4.9 %collective-permute-done.22 = bf16[128,1024]{1,0:T(8,128)(2,1)S(1)} collective-permute-done((bf16[128,1024]{1,0:T(8,128)(2,1)S(1)}, bf16[128,1024]{1,0:T(8,128)(2,1)S(1)}, u32[]{:S(2)}, u32[]{:S(2)}) %collective-permute-start.22) | collective-permute-done | bytes 262176 | tf_op jit(solution)/shard_map/ppermute | solution.py:56
  172.3 5.0 %collective-permute-done.24 = bf16[128,1024]{1,0:T(8,128)(2,1)S(1)} collective-permute-done((bf16[128,1024]{1,0:T(8,128)(2,1)S(1)}, bf16[128,1024]{1,0:T(8,128)(2,1)S(1)}, u32[]{:S(2)}, u32[]{:S(2)}) %collective-permute-start.24) | collective-permute-done | bytes 262176 | tf_op jit(solution)/shard_map/ppermute | solution.py:56
  180.4 3.0 collective-permute-start.26
  185.4 2.3 reshape.175
  190.3 4.9 %collective-permute-done.26 = bf16[128,1024]{1,0:T(8,128)(2,1)S(1)} collective-permute-done((bf16[128,1024]{1,0:T(8,128)(2,1)}, bf16[128,1024]{1,0:T(8,128)(2,1)S(1)}, u32[]{:S(2)}, u32[]{:S(2)}) %collective-permute-start.26) | collective-permute-done | bytes 262176 | tf_op jit(solution)/shard_map/ppermute | solution.py:43
  195.4 2.1 pad_maximum_fusion.8
  202.0 3.5 %convolution_convert_fusion.4 = bf16[512,1024]{1,0:T(8,128)(2,1)} fusion(bf16[576,1024]{1,0:T(8,128)(2,1)} %reshape.168, bf16[1024,640]{1,0:T(8,128)(2,1)} %copy-done.33), kind=kOutput, calls=%fused_computation.25 | convolution fusion | flops 671612928 | bytes 2883584 | tf_op jit(solution)/shard_map/dot_general | solution.py:310
  209.3 6.8 %attention_backward.1 = (bf16[1024,256]{1,0:T(8,128)(2,1)S(1)}, f32[1,256]{1,0:T(1,128)S(1)}) custom-call(s32[8]{0:T(128)S(1)} %fusion.102.place_ref, f32[1024,256]{1,0:T(8,128)S(1)} %fusion.25.proj_ref, f32[1024,128]{1,0:T(8,128)S(1)} %get-tuple-element.188.cos_ref, f32[1024,128]{1,0:T(8,128)S(1)} %get-tuple-element.189.sin_ref, ...), custom_call_target="tpu_custom_call" | custom-call | flops 3000000000 | bytes 6291456 | tf_op jit(solution)/shard_map/attention_backward/pallas_call | solution.py:264
  221.1 4.5 %all-to-all-start.1 = ((bf16[16,96,256]{2,1,0:T(8,128)(2,1)}), bf16[16,96,256]{2,1,0:T(8,128)(2,1)}, u32[]{:S(2)}, u32[]{:S(2)}) async-start(bf16[16,96,256]{2,1,0:T(8,128)(2,1)} %constant_dynamic-update-slice_fusion.51), calls=%async_computation.1 | async-start | bytes 1572864 | tf_op jit(solution)/shard_map/all_to_all | solution.py:477
  227.6 3.8 %fusion.135 = (bf16[512,1024]{1,0:T(8,128)(2,1)S(1)}, f32[512,1024]{1,0:T(8,128)}) fusion(bf16[512,1024]{1,0:T(8,128)(2,1)} %collective-permute-done.13, bf16[576,1024]{1,0:T(8,128)(2,1)S(1)} %copy-done.17, bf16[1024,640]{1,0:T(8,128)(2,1)} %copy-done.33), kind=kOutput, calls=%fused_computation.341 | convolution fusion | flops 672661504 | bytes 6029312 | tf_op jit(solution)/shard_map/dot_general | solution.py:310
  233.4 7.3 %all-to-all-done.1 = bf16[16,96,256]{2,1,0:T(8,128)(2,1)} async-done(((bf16[16,96,256]{2,1,0:T(8,128)(2,1)}), bf16[16,96,256]{2,1,0:T(8,128)(2,1)}, u32[]{:S(2)}, u32[]{:S(2)}) %all-to-all-start.1) | async-done | bytes 786464 | tf_op jit(solution)/shard_map/all_to_all | solution.py:477
  242.0 5.7 %collective-permute-start.33 = (f32[8,1024]{1,0:T(8,128)S(1)}, f32[8,1024]{1,0:T(8,128)S(1)}, u32[]{:S(2)}, u32[]{:S(2)}) collective-permute-start(f32[8,1024]{1,0:T(8,128)S(1)} %pad_maximum_fusion.15), channel_id=1, source_target_pairs={{0,0},{1,16},{2,32},{3,48},{4,64},{5,80},{6,96},{7,112},{8,1},{9,1... | collective-permute-start | bytes 98312 | tf_op jit(solution)/shard_map/ppermute | solution.py:508
  249.6 4.0 %collective-permute-start.30 = (bf16[128,1024]{1,0:T(8,128)(2,1)S(1)}, bf16[128,1024]{1,0:T(8,128)(2,1)S(1)}, u32[]{:S(2)}, u32[]{:S(2)}) collective-permute-start(bf16[128,1024]{1,0:T(8,128)(2,1)S(1)} %get-tuple-element.65), channel_id=1, source_target_pairs={{0,4},{1,5},{2,6},{3,7},{4,0},{5,1},{6,2},{7,3},{8,12},{9,13},{10,... | collective-permute-start | bytes 786440 | tf_op jit(solution)/shard_map/ppermute | solution.py:56
  257.0 3.5 %collective-permute-done.30 = bf16[128,1024]{1,0:T(8,128)(2,1)S(1)} collective-permute-done((bf16[128,1024]{1,0:T(8,128)(2,1)S(1)}, bf16[128,1024]{1,0:T(8,128)(2,1)S(1)}, u32[]{:S(2)}, u32[]{:S(2)}) %collective-permute-start.30) | collective-permute-done | bytes 262176 | tf_op jit(solution)/shard_map/ppermute | solution.py:56
  260.8 5.5 %collective-permute-done.32 = bf16[128,1024]{1,0:T(8,128)(2,1)S(1)} collective-permute-done((bf16[128,1024]{1,0:T(8,128)(2,1)S(1)}, bf16[128,1024]{1,0:T(8,128)(2,1)S(1)}, u32[]{:S(2)}, u32[]{:S(2)}) %collective-permute-start.32) | collective-permute-done | bytes 262176 | tf_op jit(solution)/shard_map/ppermute | solution.py:56
  267.4 5.4 %all-to-all-start.2 = ((f32[16,1,136]{2,1,0:T(1,128)}), f32[16,1,136]{2,1,0:T(1,128)S(1)}, u32[]{:S(2)}, u32[]{:S(2)}) async-start(f32[16,1,136]{2,1,0:T(1,128)} %reshape.172), calls=%async_computation.2 | async-start | bytes 32768 | tf_op jit(solution)/shard_map/all_to_all | solution.py:495
  272.9 6.4 %all-to-all-done.2 = f32[16,1,136]{2,1,0:T(1,128)S(1)} async-done(((f32[16,1,136]{2,1,0:T(1,128)}), f32[16,1,136]{2,1,0:T(1,128)S(1)}, u32[]{:S(2)}, u32[]{:S(2)}) %all-to-all-start.2) | async-done | bytes 8736 | tf_op jit(solution)/shard_map/all_to_all | solution.py:495
  280.1 5.3 %all-to-all-start.3 = ((f32[8,9,256]{2,1,0:T(8,128)}), f32[8,9,256]{2,1,0:T(8,128)S(1)}, u32[]{:S(2)}, u32[]{:S(2)}) async-start(f32[8,9,256]{2,1,0:T(8,128)} %select_maximum_fusion), calls=%async_computation.3 | async-start | bytes 262144 | tf_op jit(solution)/shard_map/all_to_all | solution.py:497
  285.5 2.5 fusion.30
  288.0 2.7 all-to-all-done.3
  293.6 3.6 %collective-permute-start.34 = (bf16[36,1024]{1,0:T(8,128)(2,1)S(1)}, bf16[36,1024]{1,0:T(8,128)(2,1)S(1)}, u32[]{:S(2)}, u32[]{:S(2)}) collective-permute-start(bf16[36,1024]{1,0:T(8,128)(2,1)S(1)} %pad_maximum_fusion.12), channel_id=1, source_target_pairs={{0,0},{1,16},{2,32},{3,48},{4,64},{5,80},{6,96},{7,112},{8,1},{9,1... | collective-permute-start | bytes 221192 | tf_op jit(solution)/shard_map/ppermute | solution.py:509
  304.1 5.0 %all-to-all-start.4 = ((bf16[8,8,1280]{2,1,0:T(8,128)(2,1)}), bf16[8,8,1280]{2,1,0:T(8,128)(2,1)S(1)}, u32[]{:S(2)}, u32[]{:S(2)}) async-start(bf16[8,8,1280]{2,1,0:T(8,128)(2,1)} %bitcast.60), calls=%async_computation.5 | async-start | bytes 327680 | tf_op jit(solution)/shard_map/all_to_all | solution.py:512
  310.9 3.8 %all-to-all-done.4 = bf16[8,8,1280]{2,1,0:T(8,128)(2,1)S(1)} async-done(((bf16[8,8,1280]{2,1,0:T(8,128)(2,1)}), bf16[8,8,1280]{2,1,0:T(8,128)(2,1)S(1)}, u32[]{:S(2)}, u32[]{:S(2)}) %all-to-all-start.4) | async-done | bytes 163872 | tf_op jit(solution)/shard_map/all_to_all | solution.py:512
  (327 shorter events, 96.3 us)
Async XLA Ops:
  7.2 25.2 %copy-start.11 = (bf16[128,1024]{1,0:T(8,128)(2,1)S(1)}, bf16[128,1024]{1,0:T(8,128)(2,1)}, u32[]{:S(2)}) copy-start(bf16[128,1024]{1,0:T(8,128)(2,1)} %param.18) | copy-start | bytes 786436
  7.2 25.9 %copy-start.56 = (s32[1,3]{1,0:T(1,128)S(1)}, s32[1,3]{1,0:T(1,128)}, u32[]{:S(2)}) copy-start(s32[1,3]{1,0:T(1,128)} %param.20) | copy-start | bytes 40
  7.2 54.8 %collective-permute-start.2 = (bf16[128,1024]{1,0:T(8,128)(2,1)}, bf16[128,1024]{1,0:T(8,128)(2,1)}, u32[]{:S(2)}, u32[]{:S(2)}) collective-permute-start(bf16[128,1024]{1,0:T(8,128)(2,1)} %param.18), channel_id=1, source_target_pairs={{0,2},{1,3},{2,4},{3,5},{4,6},{5,7},{6,0},{7,1},{8,10},{9,11},{10,... | collective-permute-start | bytes 786440 | tf_op jit(solution)/shard_map/ppermute | solution.py:43
  9.7 52.3 %collective-permute-start.1 = (bf16[128,1024]{1,0:T(8,128)(2,1)}, bf16[128,1024]{1,0:T(8,128)(2,1)}, u32[]{:S(2)}, u32[]{:S(2)}) collective-permute-start(bf16[128,1024]{1,0:T(8,128)(2,1)} %param.18), channel_id=1, source_target_pairs={{0,4},{1,5},{2,6},{3,7},{4,0},{5,1},{6,2},{7,3},{8,12},{9,13},{10,... | collective-permute-start | bytes 786440 | tf_op jit(solution)/shard_map/ppermute | solution.py:43
  13.0 49.0 %collective-permute-start = (bf16[128,1024]{1,0:T(8,128)(2,1)}, bf16[128,1024]{1,0:T(8,128)(2,1)}, u32[]{:S(2)}, u32[]{:S(2)}) collective-permute-start(bf16[128,1024]{1,0:T(8,128)(2,1)} %param.18), channel_id=1, source_target_pairs={{0,6},{1,7},{2,0},{3,1},{4,2},{5,3},{6,4},{7,5},{8,14},{9,15},{10,... | collective-permute-start | bytes 786440 | tf_op jit(solution)/shard_map/ppermute | solution.py:43
  16.1 23.4 %collective-permute-start.4 = (bf16[48,1024]{1,0:T(8,128)(2,1)}, bf16[48,1024]{1,0:T(8,128)(2,1)S(1)}, u32[]{:S(2)}, u32[]{:S(2)}) collective-permute-start(bf16[48,1024]{1,0:T(8,128)(2,1)} %fusion.61), channel_id=1, source_target_pairs={{0,0},{16,1},{32,2},{48,3},{64,4},{80,5},{96,6},{112,7},{1,8},{17,... | collective-permute-start | bytes 294920 | tf_op jit(solution)/shard_map/ppermute | solution.py:382
  25.5 13.0 %all-to-all-start = ((bf16[8,8,1664]{2,1,0:T(8,128)(2,1)}), bf16[8,8,1664]{2,1,0:T(8,128)(2,1)}, u32[]{:S(2)}, u32[]{:S(2)}) async-start(bf16[8,8,1664]{2,1,0:T(8,128)(2,1)} %pad_maximum_fusion.11), calls=%async_computation | async-start | bytes 425984 | tf_op jit(solution)/shard_map/all_to_all | solution.py:378
  32.4 96.5 %all-gather.4.cloned.1.call-start = ((), (), s32[]{:S(2)}) async-start(), calls=%async_computation.7 | async-start | bytes 4177920 | tf_op jit(solution)/shard_map/all_gather | solution.py:397
  40.3 252.5 %reduce-scatter.2.cloned.1.call-start = ((), (), s32[]{:S(2)}) async-start(), calls=%async_computation.6 | async-start | bytes 4177920 | tf_op jit(solution)/shard_map/reduce_scatter | solution.py:463
  63.4 9.1 %collective-permute-start.3 = (bf16[512,1024]{1,0:T(8,128)(2,1)S(1)}, bf16[512,1024]{1,0:T(8,128)(2,1)S(1)}, u32[]{:S(2)}, u32[]{:S(2)}) collective-permute-start(bf16[512,1024]{1,0:T(8,128)(2,1)S(1)} %pad_maximum_fusion.5), channel_id=1, source_target_pairs={{0,1},{1,0},{2,3},{3,2},{4,5},{5,4},{6,7},{7,6},{8,9},{9,8},{10,11... | collective-permute-start | bytes 3145736 | tf_op jit(solution)/shard_map/ppermute | solution.py:45
  80.2 3.0 collective-permute-start.5
  80.3 8.7 %collective-permute-start.19 = (bf16[128,1024]{1,0:T(8,128)(2,1)S(1)}, bf16[128,1024]{1,0:T(8,128)(2,1)S(1)}, u32[]{:S(2)}, u32[]{:S(2)}) collective-permute-start(bf16[128,1024]{1,0:T(8,128)(2,1)S(1)} %copy-done.20), channel_id=1, source_target_pairs={{0,2},{1,3},{2,4},{3,5},{4,6},{5,7},{6,0},{7,1},{8,10},{9,11},{10,... | collective-permute-start | bytes 786440 | tf_op jit(solution)/shard_map/ppermute | solution.py:43
  80.5 14.1 %collective-permute-start.18 = (bf16[128,1024]{1,0:T(8,128)(2,1)S(1)}, bf16[128,1024]{1,0:T(8,128)(2,1)S(1)}, u32[]{:S(2)}, u32[]{:S(2)}) collective-permute-start(bf16[128,1024]{1,0:T(8,128)(2,1)S(1)} %copy-done.20), channel_id=1, source_target_pairs={{0,4},{1,5},{2,6},{3,7},{4,0},{5,1},{6,2},{7,3},{8,12},{9,13},{10,... | collective-permute-start | bytes 786440 | tf_op jit(solution)/shard_map/ppermute | solution.py:43
  83.0 12.0 %collective-permute-start.17 = (bf16[128,1024]{1,0:T(8,128)(2,1)S(1)}, bf16[128,1024]{1,0:T(8,128)(2,1)S(1)}, u32[]{:S(2)}, u32[]{:S(2)}) collective-permute-start(bf16[128,1024]{1,0:T(8,128)(2,1)S(1)} %copy-done.20), channel_id=1, source_target_pairs={{0,6},{1,7},{2,0},{3,1},{4,2},{5,3},{6,4},{7,5},{8,14},{9,15},{10,... | collective-permute-start | bytes 786440 | tf_op jit(solution)/shard_map/ppermute | solution.py:43
  83.7 16.5 %collective-permute-start.6 = (bf16[128,1024]{1,0:T(8,128)(2,1)S(1)}, bf16[128,1024]{1,0:T(8,128)(2,1)S(1)}, u32[]{:S(2)}, u32[]{:S(2)}) collective-permute-start(bf16[128,1024]{1,0:T(8,128)(2,1)S(1)} %get-tuple-element.74), channel_id=1, source_target_pairs={{0,4},{1,5},{2,6},{3,7},{4,0},{5,1},{6,2},{7,3},{8,12},{9,13},{10,... | collective-permute-start | bytes 786440 | tf_op jit(solution)/shard_map/ppermute | solution.py:56
  86.0 20.2 %collective-permute-start.8 = (bf16[128,1024]{1,0:T(8,128)(2,1)S(1)}, bf16[128,1024]{1,0:T(8,128)(2,1)S(1)}, u32[]{:S(2)}, u32[]{:S(2)}) collective-permute-start(bf16[128,1024]{1,0:T(8,128)(2,1)S(1)} %get-tuple-element.75), channel_id=1, source_target_pairs={{0,6},{1,7},{2,0},{3,1},{4,2},{5,3},{6,4},{7,5},{8,14},{9,15},{10,... | collective-permute-start | bytes 786440 | tf_op jit(solution)/shard_map/ppermute | solution.py:56
  89.0 17.6 %collective-permute-start.7 = (bf16[128,1024]{1,0:T(8,128)(2,1)S(1)}, bf16[128,1024]{1,0:T(8,128)(2,1)S(1)}, u32[]{:S(2)}, u32[]{:S(2)}) collective-permute-start(bf16[128,1024]{1,0:T(8,128)(2,1)S(1)} %get-tuple-element.76), channel_id=1, source_target_pairs={{0,2},{1,3},{2,4},{3,5},{4,6},{5,7},{6,0},{7,1},{8,10},{9,11},{10,... | collective-permute-start | bytes 786440 | tf_op jit(solution)/shard_map/ppermute | solution.py:56
  95.1 30.4 %collective-permute-start.20 = (bf16[512,1024]{1,0:T(8,128)(2,1)S(1)}, bf16[512,1024]{1,0:T(8,128)(2,1)S(1)}, u32[]{:S(2)}, u32[]{:S(2)}) collective-permute-start(bf16[512,1024]{1,0:T(8,128)(2,1)S(1)} %pad_maximum_fusion.7), channel_id=1, source_target_pairs={{0,1},{1,0},{2,3},{3,2},{4,5},{5,4},{6,7},{7,6},{8,9},{9,8},{10,11... | collective-permute-start | bytes 3145736 | tf_op jit(solution)/shard_map/ppermute | solution.py:45
  107.4 71.9 %copy-start.9 = (f32[128,1024]{1,0:T(8,128)}, f32[128,1024]{1,0:T(8,128)S(1)}, u32[]{:S(2)}) copy-start(f32[128,1024]{1,0:T(8,128)S(1)} %get-tuple-element.57) | copy-start | bytes 1572868
  108.3 7.9 %collective-permute-start.11 = (bf16[128,1024]{1,0:T(8,128)(2,1)S(1)}, bf16[128,1024]{1,0:T(8,128)(2,1)S(1)}, u32[]{:S(2)}, u32[]{:S(2)}) collective-permute-start(bf16[128,1024]{1,0:T(8,128)(2,1)S(1)} %get-tuple-element.55), channel_id=1, source_target_pairs={{0,2},{1,3},{2,4},{3,5},{4,6},{5,7},{6,0},{7,1},{8,10},{9,11},{10,... | collective-permute-start | bytes 786440 | tf_op jit(solution)/shard_map/ppermute | solution.py:43
  109.0 14.5 %collective-permute-start.10 = (bf16[128,1024]{1,0:T(8,128)(2,1)S(1)}, bf16[128,1024]{1,0:T(8,128)(2,1)S(1)}, u32[]{:S(2)}, u32[]{:S(2)}) collective-permute-start(bf16[128,1024]{1,0:T(8,128)(2,1)S(1)} %get-tuple-element.55), channel_id=1, source_target_pairs={{0,4},{1,5},{2,6},{3,7},{4,0},{5,1},{6,2},{7,3},{8,12},{9,13},{10,... | collective-permute-start | bytes 786440 | tf_op jit(solution)/shard_map/ppermute | solution.py:43
  112.2 11.4 %collective-permute-start.9 = (bf16[128,1024]{1,0:T(8,128)(2,1)S(1)}, bf16[128,1024]{1,0:T(8,128)(2,1)S(1)}, u32[]{:S(2)}, u32[]{:S(2)}) collective-permute-start(bf16[128,1024]{1,0:T(8,128)(2,1)S(1)} %get-tuple-element.55), channel_id=1, source_target_pairs={{0,6},{1,7},{2,0},{3,1},{4,2},{5,3},{6,4},{7,5},{8,14},{9,15},{10,... | collective-permute-start | bytes 786440 | tf_op jit(solution)/shard_map/ppermute | solution.py:43
  123.6 4.2 %collective-permute-start.12 = (bf16[512,1024]{1,0:T(8,128)(2,1)S(1)}, bf16[512,1024]{1,0:T(8,128)(2,1)S(1)}, u32[]{:S(2)}, u32[]{:S(2)}) collective-permute-start(bf16[512,1024]{1,0:T(8,128)(2,1)S(1)} %pad_maximum_fusion.6), channel_id=1, source_target_pairs={{0,1},{1,0},{2,3},{3,2},{4,5},{5,4},{6,7},{7,6},{8,9},{9,8},{10,11... | collective-permute-start | bytes 3145736 | tf_op jit(solution)/shard_map/ppermute | solution.py:45
  153.3 8.2 %collective-permute-start.21 = (bf16[512,1024]{1,0:T(8,128)(2,1)S(1)}, bf16[512,1024]{1,0:T(8,128)(2,1)S(1)}, u32[]{:S(2)}, u32[]{:S(2)}) collective-permute-start(bf16[512,1024]{1,0:T(8,128)(2,1)S(1)} %convolution_convert_fusion.3), channel_id=1, source_target_pairs={{0,1},{1,0},{2,3},{3,2},{4,5},{5,4},{6,7},{7,6},{8,9},{9,8},{10,11... | collective-permute-start | bytes 3145736 | tf_op jit(solution)/shard_map/ppermute | solution.py:51
  163.1 9.3 %collective-permute-start.22 = (bf16[128,1024]{1,0:T(8,128)(2,1)S(1)}, bf16[128,1024]{1,0:T(8,128)(2,1)S(1)}, u32[]{:S(2)}, u32[]{:S(2)}) collective-permute-start(bf16[128,1024]{1,0:T(8,128)(2,1)S(1)} %get-tuple-element.68), channel_id=1, source_target_pairs={{0,4},{1,5},{2,6},{3,7},{4,0},{5,1},{6,2},{7,3},{8,12},{9,13},{10,... | collective-permute-start | bytes 786440 | tf_op jit(solution)/shard_map/ppermute | solution.py:56
  163.6 13.7 %collective-permute-start.24 = (bf16[128,1024]{1,0:T(8,128)(2,1)S(1)}, bf16[128,1024]{1,0:T(8,128)(2,1)S(1)}, u32[]{:S(2)}, u32[]{:S(2)}) collective-permute-start(bf16[128,1024]{1,0:T(8,128)(2,1)S(1)} %get-tuple-element.69), channel_id=1, source_target_pairs={{0,6},{1,7},{2,0},{3,1},{4,2},{5,3},{6,4},{7,5},{8,14},{9,15},{10,... | collective-permute-start | bytes 786440 | tf_op jit(solution)/shard_map/ppermute | solution.py:56
  165.4 13.1 %collective-permute-start.23 = (bf16[128,1024]{1,0:T(8,128)(2,1)S(1)}, bf16[128,1024]{1,0:T(8,128)(2,1)S(1)}, u32[]{:S(2)}, u32[]{:S(2)}) collective-permute-start(bf16[128,1024]{1,0:T(8,128)(2,1)S(1)} %get-tuple-element.70), channel_id=1, source_target_pairs={{0,2},{1,3},{2,4},{3,5},{4,6},{5,7},{6,0},{7,1},{8,10},{9,11},{10,... | collective-permute-start | bytes 786440 | tf_op jit(solution)/shard_map/ppermute | solution.py:56
  180.4 9.9 %collective-permute-start.27 = (bf16[128,1024]{1,0:T(8,128)(2,1)}, bf16[128,1024]{1,0:T(8,128)(2,1)S(1)}, u32[]{:S(2)}, u32[]{:S(2)}) collective-permute-start(bf16[128,1024]{1,0:T(8,128)(2,1)} %get-tuple-element.52), channel_id=1, source_target_pairs={{0,2},{1,3},{2,4},{3,5},{4,6},{5,7},{6,0},{7,1},{8,10},{9,11},{10,... | collective-permute-start | bytes 786440 | tf_op jit(solution)/shard_map/ppermute | solution.py:43
  180.4 14.7 %collective-permute-start.26 = (bf16[128,1024]{1,0:T(8,128)(2,1)}, bf16[128,1024]{1,0:T(8,128)(2,1)S(1)}, u32[]{:S(2)}, u32[]{:S(2)}) collective-permute-start(bf16[128,1024]{1,0:T(8,128)(2,1)} %get-tuple-element.52), channel_id=1, source_target_pairs={{0,4},{1,5},{2,6},{3,7},{4,0},{5,1},{6,2},{7,3},{8,12},{9,13},{10,... | collective-permute-start | bytes 786440 | tf_op jit(solution)/shard_map/ppermute | solution.py:43
  183.4 12.0 %collective-permute-start.25 = (bf16[128,1024]{1,0:T(8,128)(2,1)}, bf16[128,1024]{1,0:T(8,128)(2,1)}, u32[]{:S(2)}, u32[]{:S(2)}) collective-permute-start(bf16[128,1024]{1,0:T(8,128)(2,1)} %get-tuple-element.52), channel_id=1, source_target_pairs={{0,6},{1,7},{2,0},{3,1},{4,2},{5,3},{6,4},{7,5},{8,14},{9,15},{10,... | collective-permute-start | bytes 786440 | tf_op jit(solution)/shard_map/ppermute | solution.py:43
  197.4 9.1 %collective-permute-start.28 = (bf16[512,1024]{1,0:T(8,128)(2,1)}, bf16[512,1024]{1,0:T(8,128)(2,1)}, u32[]{:S(2)}, u32[]{:S(2)}) collective-permute-start(bf16[512,1024]{1,0:T(8,128)(2,1)} %pad_maximum_fusion.8), channel_id=1, source_target_pairs={{0,1},{1,0},{2,3},{3,2},{4,5},{5,4},{6,7},{7,6},{8,9},{9,8},{10,11... | collective-permute-start | bytes 3145736 | tf_op jit(solution)/shard_map/ppermute | solution.py:45
  205.4 22.1 %collective-permute-start.13 = (bf16[512,1024]{1,0:T(8,128)(2,1)}, bf16[512,1024]{1,0:T(8,128)(2,1)}, u32[]{:S(2)}, u32[]{:S(2)}) collective-permute-start(bf16[512,1024]{1,0:T(8,128)(2,1)} %convolution_convert_fusion.4), channel_id=1, source_target_pairs={{0,1},{1,0},{2,3},{3,2},{4,5},{5,4},{6,7},{7,6},{8,9},{9,8},{10,11... | collective-permute-start | bytes 3145736 | tf_op jit(solution)/shard_map/ppermute | solution.py:51
  221.1 19.6 %all-to-all-start.1 = ((bf16[16,96,256]{2,1,0:T(8,128)(2,1)}), bf16[16,96,256]{2,1,0:T(8,128)(2,1)}, u32[]{:S(2)}, u32[]{:S(2)}) async-start(bf16[16,96,256]{2,1,0:T(8,128)(2,1)} %constant_dynamic-update-slice_fusion.51), calls=%async_computation.1 | async-start | bytes 1572864 | tf_op jit(solution)/shard_map/all_to_all | solution.py:477
  227.1 20.6 %collective-permute-start.29 = (bf16[512,1024]{1,0:T(8,128)(2,1)}, bf16[512,1024]{1,0:T(8,128)(2,1)}, u32[]{:S(2)}, u32[]{:S(2)}) collective-permute-start(bf16[512,1024]{1,0:T(8,128)(2,1)} %convolution_convert_fusion.2), channel_id=1, source_target_pairs={{0,1},{1,0},{2,3},{3,2},{4,5},{5,4},{6,7},{7,6},{8,9},{9,8},{10,11... | collective-permute-start | bytes 3145736 | tf_op jit(solution)/shard_map/ppermute | solution.py:51
  232.3 53.1 %collective-permute-start.14 = (bf16[128,1024]{1,0:T(8,128)(2,1)}, bf16[128,1024]{1,0:T(8,128)(2,1)S(1)}, u32[]{:S(2)}, u32[]{:S(2)}) collective-permute-start(bf16[128,1024]{1,0:T(8,128)(2,1)} %get-tuple-element.71), channel_id=1, source_target_pairs={{0,4},{1,5},{2,6},{3,7},{4,0},{5,1},{6,2},{7,3},{8,12},{9,13},{10,... | collective-permute-start | bytes 786440 | tf_op jit(solution)/shard_map/ppermute | solution.py:56
  242.0 13.1 %collective-permute-start.33 = (f32[8,1024]{1,0:T(8,128)S(1)}, f32[8,1024]{1,0:T(8,128)S(1)}, u32[]{:S(2)}, u32[]{:S(2)}) collective-permute-start(f32[8,1024]{1,0:T(8,128)S(1)} %pad_maximum_fusion.15), channel_id=1, source_target_pairs={{0,0},{1,16},{2,32},{3,48},{4,64},{5,80},{6,96},{7,112},{8,1},{9,1... | collective-permute-start | bytes 98312 | tf_op jit(solution)/shard_map/ppermute | solution.py:508
  249.5 36.0 %copy-start.10 = (f32[128,1024]{1,0:T(8,128)S(1)}, f32[128,1024]{1,0:T(8,128)}, u32[]{:S(2)}) copy-start(f32[128,1024]{1,0:T(8,128)} %copy-done.9) | copy-start | bytes 1572868
  249.5 35.9 %copy-start.19 = (f32[128,1024]{1,0:T(8,128)S(1)}, f32[128,1024]{1,0:T(8,128)}, u32[]{:S(2)}) copy-start(f32[128,1024]{1,0:T(8,128)} %copy-done.18) | copy-start | bytes 1572868
  249.5 35.9 %copy-start.22 = (bf16[128,1024]{1,0:T(8,128)(2,1)S(1)}, bf16[128,1024]{1,0:T(8,128)(2,1)}, u32[]{:S(2)}) copy-start(bf16[128,1024]{1,0:T(8,128)(2,1)} %param.19) | copy-start | bytes 786436
  249.6 10.9 %collective-permute-start.30 = (bf16[128,1024]{1,0:T(8,128)(2,1)S(1)}, bf16[128,1024]{1,0:T(8,128)(2,1)S(1)}, u32[]{:S(2)}, u32[]{:S(2)}) collective-permute-start(bf16[128,1024]{1,0:T(8,128)(2,1)S(1)} %get-tuple-element.65), channel_id=1, source_target_pairs={{0,4},{1,5},{2,6},{3,7},{4,0},{5,1},{6,2},{7,3},{8,12},{9,13},{10,... | collective-permute-start | bytes 786440 | tf_op jit(solution)/shard_map/ppermute | solution.py:56
  253.6 12.7 %collective-permute-start.32 = (bf16[128,1024]{1,0:T(8,128)(2,1)S(1)}, bf16[128,1024]{1,0:T(8,128)(2,1)S(1)}, u32[]{:S(2)}, u32[]{:S(2)}) collective-permute-start(bf16[128,1024]{1,0:T(8,128)(2,1)S(1)} %get-tuple-element.66), channel_id=1, source_target_pairs={{0,6},{1,7},{2,0},{3,1},{4,2},{5,3},{6,4},{7,5},{8,14},{9,15},{10,... | collective-permute-start | bytes 786440 | tf_op jit(solution)/shard_map/ppermute | solution.py:56
  253.6 12.7 %collective-permute-start.31 = (bf16[128,1024]{1,0:T(8,128)(2,1)S(1)}, bf16[128,1024]{1,0:T(8,128)(2,1)S(1)}, u32[]{:S(2)}, u32[]{:S(2)}) collective-permute-start(bf16[128,1024]{1,0:T(8,128)(2,1)S(1)} %get-tuple-element.67), channel_id=1, source_target_pairs={{0,2},{1,3},{2,4},{3,5},{4,6},{5,7},{6,0},{7,1},{8,10},{9,11},{10,... | collective-permute-start | bytes 786440 | tf_op jit(solution)/shard_map/ppermute | solution.py:56
  255.1 30.3 %collective-permute-start.16 = (bf16[128,1024]{1,0:T(8,128)(2,1)}, bf16[128,1024]{1,0:T(8,128)(2,1)S(1)}, u32[]{:S(2)}, u32[]{:S(2)}) collective-permute-start(bf16[128,1024]{1,0:T(8,128)(2,1)} %get-tuple-element.72), channel_id=1, source_target_pairs={{0,6},{1,7},{2,0},{3,1},{4,2},{5,3},{6,4},{7,5},{8,14},{9,15},{10,... | collective-permute-start | bytes 786440 | tf_op jit(solution)/shard_map/ppermute | solution.py:56
  260.5 24.9 %collective-permute-start.15 = (bf16[128,1024]{1,0:T(8,128)(2,1)}, bf16[128,1024]{1,0:T(8,128)(2,1)S(1)}, u32[]{:S(2)}, u32[]{:S(2)}) collective-permute-start(bf16[128,1024]{1,0:T(8,128)(2,1)} %get-tuple-element.73), channel_id=1, source_target_pairs={{0,2},{1,3},{2,4},{3,5},{4,6},{5,7},{6,0},{7,1},{8,10},{9,11},{10,... | collective-permute-start | bytes 786440 | tf_op jit(solution)/shard_map/ppermute | solution.py:56
  267.4 11.9 %all-to-all-start.2 = ((f32[16,1,136]{2,1,0:T(1,128)}), f32[16,1,136]{2,1,0:T(1,128)S(1)}, u32[]{:S(2)}, u32[]{:S(2)}) async-start(f32[16,1,136]{2,1,0:T(1,128)} %reshape.172), calls=%async_computation.2 | async-start | bytes 32768 | tf_op jit(solution)/shard_map/all_to_all | solution.py:495
  280.1 10.6 %all-to-all-start.3 = ((f32[8,9,256]{2,1,0:T(8,128)}), f32[8,9,256]{2,1,0:T(8,128)S(1)}, u32[]{:S(2)}, u32[]{:S(2)}) async-start(f32[8,9,256]{2,1,0:T(8,128)} %select_maximum_fusion), calls=%async_computation.3 | async-start | bytes 262144 | tf_op jit(solution)/shard_map/all_to_all | solution.py:497
  293.6 15.5 %collective-permute-start.34 = (bf16[36,1024]{1,0:T(8,128)(2,1)S(1)}, bf16[36,1024]{1,0:T(8,128)(2,1)S(1)}, u32[]{:S(2)}, u32[]{:S(2)}) collective-permute-start(bf16[36,1024]{1,0:T(8,128)(2,1)S(1)} %pad_maximum_fusion.12), channel_id=1, source_target_pairs={{0,0},{1,16},{2,32},{3,48},{4,64},{5,80},{6,96},{7,112},{8,1},{9,1... | collective-permute-start | bytes 221192 | tf_op jit(solution)/shard_map/ppermute | solution.py:509
  304.1 10.5 %all-to-all-start.4 = ((bf16[8,8,1280]{2,1,0:T(8,128)(2,1)}), bf16[8,8,1280]{2,1,0:T(8,128)(2,1)S(1)}, u32[]{:S(2)}, u32[]{:S(2)}) async-start(bf16[8,8,1280]{2,1,0:T(8,128)(2,1)} %bitcast.60), calls=%async_computation.5 | async-start | bytes 327680 | tf_op jit(solution)/shard_map/all_to_all | solution.py:512
  (52 other events, 493.8 us)
Sparse Core Ops, SparseCore 0:
  40.5 47.9 all-gather.3
  200.7 77.7 reduce-scatter.1
